TPU v7x, 256 devices: a whole 4x4x8 slice. The times are simulated.
256 devices in a mesh: row: 8 (over y, z_hi), col: 8 (over x, core), pack: 4 (over z_lo).
Axes of the slice: x: 4, y: 4, z: 8 (z_hi: 2, z_lo: 4; z = z_hi * 4 + z_lo), core: 2. Of those that a mesh axis runs over, the one named last changes fastest.
Arguments:
- giant_emb: bfloat16 [32768, 1024], P(('row', 'col', 'pack')), may hold values from -8 to 8
- small_emb: bfloat16 [262144, 1024], P(('row', 'col', 'pack')), may hold values from -8 to 8
- small_ids: int32 [262144], P(('row', 'col', 'pack')), may hold values from 0 to 128, as said below
- send_rows: int32 [32768], P(('row', 'col', 'pack')), may hold values from 0 to 1023
- target_rows: int32 [32768], P(('row', 'col', 'pack')), may hold values from 0 to 1023, as said below
Outputs:
- giant_max: float32 [32768], P(('row', 'col', 'pack'))
- small_max: float32 [262144], P(('row', 'col', 'pack'))
Inputs may be any that keep to these rules, and one draw needn't show every extreme that they name: `small_ids`: within each block of 1024 rows the ids are nondecreasing, so members of one cluster are contiguous. `target_rows`: the 128 entries of one block are distinct.
All inputs are finite; a program needn't handle non-finite values.
Results may differ from a plain program's by a relative error of at most 0.002.
Values may be sent and summed in bfloat16 or wider, within the bound.
No kernel may reach another device: no remote copies, remote signals or barrier semaphores. Data moves between devices by JAX's collectives and lax.ppermute only.
A program may use at most 64 MiB of HBM per device.

v0:
```python
import jax
import jax.numpy as jnp
from jax import lax
from jax.sharding import PartitionSpec as P


def shifted(block, axis, distance):
    devices = range(lax.axis_size(axis))
    route = [((i - distance) % len(devices), i) for i in devices]
    return lax.ppermute(block, axis, route)


def to_unit(values):
    wide = values.astype(jnp.float32)
    inverse = lax.rsqrt(jnp.sum(wide * wide, axis=-1, keepdims=True) + 1e-06)
    return (wide * inverse).astype(jnp.bfloat16)


def body(giant_emb, small_emb, small_ids, send_rows, target_rows):
    shard_rows = giant_emb.shape[0]
    n_col = lax.axis_size("col")
    n_pack = lax.axis_size("pack")
    row_index = lax.axis_index("row")
    col_index = lax.axis_index("col")
    pack_index = lax.axis_index("pack")
    unit_rows = to_unit(giant_emb)
    row_panel = lax.all_gather(unit_rows, "col", axis=0, tiled=True)
    panel_pos = jnp.arange(n_col * shard_rows, dtype=jnp.int32)
    row_global = (
        (row_index * n_col + panel_pos // shard_rows) * n_pack + pack_index
    ) * shard_rows + panel_pos % shard_rows
    initial_max = jnp.full((n_col * shard_rows,), -1.0, jnp.float32)
    column_block = lax.all_gather(unit_rows, ("row", "pack"), axis=0, tiled=True)
    piece_rows = column_block.shape[0]
    gathered_pos = jnp.arange(piece_rows, dtype=jnp.int32)
    shard_pos = gathered_pos // shard_rows
    col_global = (
        (shard_pos // n_pack * n_col + col_index) * n_pack + shard_pos % n_pack
    ) * shard_rows + gathered_pos % shard_rows
    scores = jnp.einsum("kd,qd->kq", column_block, row_panel, preferred_element_type=jnp.float32)
    allowed = col_global[:, None] < row_global[None, :]
    masked = jnp.where(allowed, scores, jnp.float32(-1.0))
    best_rows = jnp.maximum(initial_max, jnp.max(masked, axis=0))
    whole_panel = lax.pmax(best_rows, "col")
    giant_max = lax.dynamic_slice_in_dim(whole_panel, col_index * shard_rows, shard_rows, 0)
    small_unit = to_unit(small_emb)
    block_size = small_unit.shape[0]
    outgoing = jnp.take(small_unit, send_rows, axis=0)
    incoming = shifted(outgoing, "pack", 1)
    member_pos = jnp.arange(block_size, dtype=jnp.int32)
    local_scores = jnp.einsum(
        "id,jd->ij", small_unit, small_unit, preferred_element_type=jnp.float32
    )
    local_allowed = (small_ids[:, None] == small_ids[None, :]) & (
        member_pos[None, :] < member_pos[:, None]
    )
    local_max = jnp.max(jnp.where(local_allowed, local_scores, jnp.float32(-1.0)), axis=1)
    cross = jnp.einsum("td,id->ti", incoming, small_unit, preferred_element_type=jnp.float32)
    target_ids = jnp.take(small_ids, target_rows)
    cross = jnp.where(target_ids[:, None] == small_ids[None, :], cross, jnp.float32(-1.0))
    toward_max = jnp.max(cross, axis=0)
    back_max = jnp.max(cross, axis=1)
    returned = shifted(back_max, "pack", -1)
    hits = send_rows[:, None] == member_pos[None, :]
    returned_max = jnp.max(jnp.where(hits, returned[:, None], jnp.float32(-1.0)), axis=0)
    small_max = jnp.maximum(jnp.maximum(local_max, toward_max), returned_max)
    return (giant_max, small_max)


def solution(mesh):
    in_specs = (
        P(("row", "col", "pack"), None),
        P(("row", "col", "pack"), None),
        P(("row", "col", "pack")),
        P(("row", "col", "pack")),
        P(("row", "col", "pack")),
    )
    out_specs = (P(("row", "col", "pack")), P(("row", "col", "pack")))
    return jax.shard_map(body, mesh=mesh, in_specs=in_specs, out_specs=out_specs, check_vma=False)
```

profile of v0, /device:TPU:1, one launch (start us, length us, event | category | flops | bytes accessed | tf_op | source)
XLA Modules:
  0.0 175.3 jit_solution(8644198531767256758)
XLA Ops:
  7.2 0.0 all-gather.5.cloned.1.call-start
  7.2 1.1 fusion.3
  8.3 1.8 %fusion.4 = bf16[128,1024]{1,0:T(8,128)(2,1)} fusion(bf16[128,1024]{1,0:T(8,128)(2,1)} %param.5, f32[128]{0:T(128)S(1)} %add_rsqrt_fusion.1), kind=kLoop, calls=%fused_computation.14 | loop fusion | flops 393216 | bytes 524800 | tf_op jit(solution)/shard_map/convert_element_type | solution.py:16
  10.1 0.0 all-gather.3.cloned.1.call-start
  10.2 0.7 all-gather.3.cloned.1.call-update
  10.9 0.7 compare_select_fusion
  11.6 2.1 %fusion = f32[1024]{0:T(1024)S(1)} fusion(bf16[1024,1024]{1,0:T(8,128)(2,1)} %param.6), kind=kLoop, calls=%fused_computation.5 | loop fusion | flops 3144704 | bytes 2101248 | tf_op jit(solution)/shard_map/reduce_sum | solution.py:15
  13.7 2.0 %fusion.1 = bf16[1024,1024]{1,0:T(8,128)(2,1)S(1)} fusion(bf16[1024,1024]{1,0:T(8,128)(2,1)} %param.6, f32[1024]{0:T(1024)S(1)} %add_rsqrt_fusion), kind=kLoop, calls=%fused_computation.6 | loop fusion | flops 3145728 | bytes 4198400 | tf_op jit(solution)/shard_map/convert_element_type | solution.py:16
  15.7 0.9 gather_fusion.1
  16.5 0.1 broadcast_select_fusion
  16.6 2.5 %collective-permute-start = (bf16[128,1024]{1,0:T(8,128)(2,1)S(1)}, bf16[128,1024]{1,0:T(8,128)(2,1)S(1)}, u32[]{:S(2)}, u32[]{:S(2)}) collective-permute-start(bf16[128,1024]{1,0:T(8,128)(2,1)S(1)} %broadcast_select_fusion), channel_id=1, source_target_pairs={{3,0},{0,1},{1,2},{2,3},{7,4},{4,5},{5,6},{6,7},{11,8},{8,9},{9,10... | collective-permute-start | bytes 786440 | tf_op jit(solution)/shard_map/ppermute | solution.py:10
  19.2 2.5 %select_reduce_fusion.1 = f32[1024]{0:T(1024)S(1)} fusion(s32[1024]{0:T(1024)S(1)} %copy-done, bf16[1024,1024]{1,0:T(8,128)(2,1)S(1)} %fusion.1), kind=kOutput, calls=%fused_computation.7 | convolution fusion | flops 2152725504 | bytes 2105344 | tf_op jit(solution)/shard_map/id,jd->ij/dot_general | solution.py:51
  21.8 1.0 gather_fusion
  22.7 4.2 %collective-permute-done = bf16[128,1024]{1,0:T(8,128)(2,1)S(1)} collective-permute-done((bf16[128,1024]{1,0:T(8,128)(2,1)S(1)}, bf16[128,1024]{1,0:T(8,128)(2,1)S(1)}, u32[]{:S(2)}, u32[]{:S(2)}) %collective-permute-start) | collective-permute-done | bytes 262176 | tf_op jit(solution)/shard_map/ppermute | solution.py:10
  26.9 0.9 fusion.37
  27.8 2.2 %collective-permute-start.1 = (f32[128]{0:T(128)S(1)}, f32[128]{0:T(128)S(1)}, u32[]{:S(2)}, u32[]{:S(2)}) collective-permute-start(f32[128]{0:T(128)S(1)} %get-tuple-element.3), channel_id=1, source_target_pairs={{1,0},{2,1},{3,2},{0,3},{5,4},{6,5},{7,6},{4,7},{9,8},{10,9},{11,1... | collective-permute-start | bytes 1544 | tf_op jit(solution)/shard_map/ppermute | solution.py:10
  30.1 0.7 collective-permute-done.1
  30.8 0.1 select_reduce_fusion.2
  30.9 0.6 maximum_maximum_fusion
  31.5 10.7 %all-gather.5.cloned.1.call-done = bf16[1024,1024]{1,0:T(8,128)(2,1)} async-done(((bf16[128,1024]{1,0:T(8,128)(2,1)}), bf16[1024,1024]{1,0:T(8,128)(2,1)}) %all-gather.5.cloned.1.call-update) | async-done | bytes 2097168 | tf_op jit(solution)/shard_map/all_gather | solution.py:27
  42.2 100.7 %all-gather.3.cloned.1.call-done = bf16[4096,1024]{1,0:T(8,128)(2,1)} async-done(((bf16[128,1024]{1,0:T(8,128)(2,1)}), bf16[4096,1024]{1,0:T(8,128)(2,1)}) %all-gather.3.cloned.1.call-update) | async-done | bytes 8388624 | tf_op jit(solution)/shard_map/all_gather | solution.py:33
  142.8 12.2 %select_reduce_fusion = f32[1024]{0:T(1024)S(1)} fusion(s32[1024]{0:T(1024)S(1)} %fusion.35, s32[4096]{0:T(1024)S(1)} %fusion.16, bf16[4096,1024]{1,0:T(8,128)(2,1)} %all-gather.3.cloned.1.call-done, bf16[1024,1024]{1,0:T(8,128)(2,1)} %all-gather.5.cloned.1.call-done), kind=kOutput, calls=%fused_computation.2 | convolution fusion | flops 8602516480 | bytes 10510336 | tf_op jit(solution)/shard_map/kd,qd->kq/dot_general | solution.py:40
  155.1 12.9 %pmax.7 = f32[1024]{0:T(1024)S(1)} all-reduce(f32[1024]{0:T(1024)S(1)} %broadcast_maximum_fusion), channel_id=1, replica_groups=mesh['row'=8,'col'=8,'pack'=4] {'col'}, use_global_device_ids=true, to_apply=%region_2.3 | all-reduce | flops 1024 | bytes 8192 | tf_op jit(solution)/shard_map/pmax | solution.py:44
  167.9 0.6 dynamic_slice.3
  (17 shorter events, 0.1 us)
Async XLA Ops:
  7.2 35.0 %all-gather.5.cloned.1.call-start = ((), (), s32[]{:S(2)}) async-start(), calls=%async_computation.1 | async-start | bytes 2359296 | tf_op jit(solution)/shard_map/all_gather | solution.py:27
  10.1 132.7 %all-gather.3.cloned.1.call-start = ((), (), s32[]{:S(2)}) async-start(), calls=%async_computation | async-start | bytes 8650752 | tf_op jit(solution)/shard_map/all_gather | solution.py:33
  11.5 5.0 %copy-start.1 = (s32[128]{0:T(128)S(1)}, s32[128]{0:T(128)}, u32[]{:S(2)}) copy-start(s32[128]{0:T(128)} %param.8) | copy-start | bytes 1540
  11.5 7.7 %copy-start.2 = (s32[128]{0:T(128)S(1)}, s32[128]{0:T(128)}, u32[]{:S(2)}) copy-start(s32[128]{0:T(128)} %param.9) | copy-start | bytes 1540
  11.6 7.7 %copy-start = (s32[1024]{0:T(1024)S(1)}, s32[1024]{0:T(1024)}, u32[]{:S(2)}) copy-start(s32[1024]{0:T(1024)} %param.7) | copy-start | bytes 12292
  16.6 10.3 %collective-permute-start = (bf16[128,1024]{1,0:T(8,128)(2,1)S(1)}, bf16[128,1024]{1,0:T(8,128)(2,1)S(1)}, u32[]{:S(2)}, u32[]{:S(2)}) collective-permute-start(bf16[128,1024]{1,0:T(8,128)(2,1)S(1)} %broadcast_select_fusion), channel_id=1, source_target_pairs={{3,0},{0,1},{1,2},{2,3},{7,4},{4,5},{5,6},{6,7},{11,8},{8,9},{9,10... | collective-permute-start | bytes 786440 | tf_op jit(solution)/shard_map/ppermute | solution.py:10
  27.8 3.0 %collective-permute-start.1 = (f32[128]{0:T(128)S(1)}, f32[128]{0:T(128)S(1)}, u32[]{:S(2)}, u32[]{:S(2)}) collective-permute-start(f32[128]{0:T(128)S(1)} %get-tuple-element.3), channel_id=1, source_target_pairs={{1,0},{2,1},{3,2},{0,3},{5,4},{6,5},{7,6},{4,7},{9,8},{10,9},{11,1... | collective-permute-start | bytes 1544 | tf_op jit(solution)/shard_map/ppermute | solution.py:10
Sparse Core Ops, SparseCore 0:
  10.2 31.8 all-gather.4
  44.8 98.0 all-gather.2
where the time goes:
time: 176 us; the launch traced here: 175 us
  waiting for transfers between devices  117 us (66%)
  matrix products  15.6 us (9%)
  between operations  14.2 us (8%)
  blocking collectives  12.9 us (7%)
  other arithmetic  8.49 us (5%)
  starting transfers between devices  4.86 us (3%)
  local copies, waits for them, and re-layouts  2.44 us (1%)
    all_gather x1, waiting for transfers between devices, body(): lax.all_gather(unit_rows, ('row', 'pack'), axis=0, tiled=True)  101 us
    pmax x1, blocking collectives, body(): whole_panel = lax.pmax(best_rows, 'col')  12.9 us
    dot_general x1, matrix products, body(): jnp.einsum('kd,qd->kq', column_block, row_panel, preferred_element_type=j...  12.2 us
    all_gather x1, waiting for transfers between devices, body(): row_panel = lax.all_gather(unit_rows, 'col', axis=0, tiled=True)  10.7 us
    ppermute x2, waiting for transfers between devices, shifted(): return lax.ppermute(block, axis, route)  4.88 us
    ppermute x2, starting transfers between devices, shifted(): return lax.ppermute(block, axis, route)  4.78 us
    convert_element_type x2, other arithmetic, to_unit(): return (wide * inverse).astype(jnp.bfloat16)  3.78 us
  transfers between devices with their start and end apart: 4, of which 4 were waited for; matrix products, arithmetic and copies ran while one was open for 6% of the time, Pallas kernels for 0%

commit v1 on v0

v1 whole, which is shorter than its diff:
```python
import functools
import jax
import jax.numpy as jnp
from jax import lax
from jax.experimental import pallas as pl
from jax.experimental.pallas import tpu as pltpu
from jax.sharding import PartitionSpec as P

AXES = ("row", "col", "pack")
LOW = -2.0
NT = (((1,), (1,)), ((), ()))


def place(x, y, z, c):
    return ((y * 2 + z // 4) * 8 + x * 2 + c) * 4 + z % 4


def z_even(x, y, z):
    return x, y, z ^ 1


def z_odd(x, y, z):
    return x, y, ((z + 7) % 8 if z % 2 == 0 else (z + 1) % 8)


MOVES = {
    "x0": lambda x, y, z: (x ^ 1, y, z),
    "x1": lambda x, y, z: (x ^ 3, y, z),
    "y0": lambda x, y, z: (x, y ^ 1, z),
    "y1": lambda x, y, z: (x, y ^ 3, z),
    "z0": z_even,
    "z1": z_odd,
}
ORDER = {
    "a": (("x0", "y0", "x1", "y1"), ("y0", "x0", "y1", "x1")),
    "b": (("x1", "y1", "x0", "y0"), ("y1", "x1", "y0", "x0")),
    "z": (("z0", "z1", "z0", "z1"), ("z1", "z0", "z1", "z0")),
}


def exchange(block, stream, step):
    route = []
    for x in range(4):
        for y in range(4):
            for z in range(8):
                for c in range(2):
                    to = MOVES[ORDER[stream][c][step]](x, y, z)
                    route.append((place(x, y, z, c), place(*to, c)))
    return lax.ppermute(block, AXES, route)


def core_swap(block):
    route = [
        (place(x, y, z, c), place(x, y, z, 1 - c))
        for x in range(4) for y in range(4) for z in range(8) for c in range(2)
    ]
    return lax.ppermute(block, AXES, route)


def unit_kernel(values_ref, out_ref):
    wide = values_ref[...].astype(jnp.float32)
    inverse = lax.rsqrt(jnp.sum(wide * wide, axis=-1, keepdims=True) + 1e-06)
    out_ref[...] = (wide * inverse).astype(jnp.bfloat16)


def unit_call(values):
    return pl.pallas_call(
        unit_kernel,
        out_shape=jax.ShapeDtypeStruct(values.shape, jnp.bfloat16),
        in_specs=[pl.BlockSpec(memory_space=pltpu.VMEM)],
        out_specs=pl.BlockSpec(memory_space=pltpu.VMEM),
        compiler_params=pltpu.CompilerParams(vmem_limit_bytes=32 * 1024 * 1024),
    )(values)


def tile_kernel(n_r, n_c, r_starts, c_starts, *refs):
    r_refs, c_refs, out_ref = refs[:n_r], refs[n_r : n_r + n_c], refs[-1]
    lane = lax.broadcasted_iota(jnp.int32, (1, 256), 1)
    sub = lax.broadcasted_iota(jnp.int32, (128, 256), 0)
    base = 0
    for r_ref in r_refs:
        for j in range(r_ref.shape[0] // 256):
            rows = r_ref[256 * j : 256 * (j + 1), :]
            first = (base + 256 * j) // 64
            row_pos = r_starts[first] + lane
            for k in range(1, 4):
                row_pos = jnp.where(lane >= 64 * k, r_starts[first + k] + lane - 64 * k, row_pos)
            best = jnp.full((8, 256), LOW, jnp.float32)
            for i, c_ref in enumerate(c_refs):
                scores = lax.dot_general(c_ref[...], rows, NT, preferred_element_type=jnp.float32)
                for h in range(2):
                    limit = row_pos - c_starts[2 * i + h]
                    part = jnp.where(sub < limit, scores[128 * h : 128 * (h + 1)], LOW)
                    best = jnp.maximum(best, jnp.max(part.reshape(16, 8, 256), axis=0))
            out_ref[:, base + 256 * j : base + 256 * (j + 1)] = jnp.max(best, axis=0, keepdims=True)
        base += r_ref.shape[0]


def tile_max(r_list, r_starts, c_list, c_starts):
    rows = sum(r.shape[0] for r in r_list)
    cols = sum(c.shape[0] for c in c_list)
    smem = pl.BlockSpec(memory_space=pltpu.SMEM)
    vmem = pl.BlockSpec(memory_space=pltpu.VMEM)
    return pl.pallas_call(
        functools.partial(tile_kernel, len(r_list), len(c_list)),
        out_shape=jax.ShapeDtypeStruct((1, rows), jnp.float32),
        in_specs=[smem, smem] + [vmem] * (len(r_list) + len(c_list)),
        out_specs=vmem,
        compiler_params=pltpu.CompilerParams(vmem_limit_bytes=40 * 1024 * 1024),
        cost_estimate=pl.CostEstimate(
            flops=2 * rows * cols * 1024, bytes_accessed=(rows + cols) * 2048, transcendentals=0
        ),
    )(r_starts, c_starts, *r_list, *c_list)


def giant_part(giant_emb):
    rows = giant_emb.shape[0]
    half = rows // 2
    row_index, col_index, z_low = (lax.axis_index(a) for a in AXES)
    x, core = col_index // 2, col_index % 2
    y, z = row_index // 2, (row_index % 2) * 4 + z_low
    unit = unit_call(giant_emb)

    spot = jnp.arange(16, dtype=jnp.int32)
    bit = [(spot >> k) & 1 for k in range(4)]

    def plane_starts(x_bits, y_bits):
        xs = x ^ bit[x_bits[0]] ^ (3 * bit[x_bits[1]])
        ys = y ^ bit[y_bits[0]] ^ (3 * bit[y_bits[1]])
        return place(xs, ys, z, core) * rows

    first = core == 0
    a_starts = jnp.where(first, plane_starts((0, 2), (1, 3)), plane_starts((1, 3), (0, 2)))
    b_starts = jnp.where(first, plane_starts((2, 0), (3, 1)), plane_starts((3, 1), (2, 0))) + half

    def line_starts(zz, cc):
        def step(v, odd):
            up = (v % 2 == 0) != odd
            return jnp.where(up, (v + 1) % 8, (v + 7) % 8)
        o0 = cc == 1
        o1 = cc == 0
        z1 = step(zz, o0)
        q = step(zz, o1)
        r = step(z1, o1)
        s = step(step(q, o0), o1)
        order = [zz, z1, q, step(q, o0), r, step(r, o0), s, step(s, o0)]
        return jnp.stack([place(x, y, v, cc) * rows for v in order])

    own_starts, other_starts = line_starts(z, core), line_starts(z, 1 - core)

    a, b = unit[:half], unit[half:]
    a1, b1, c1 = exchange(a, "a", 0), exchange(b, "b", 0), exchange(unit, "z", 0)
    a, b, c01 = jnp.concatenate([a, a1]), jnp.concatenate([b, b1]), jnp.concatenate([unit, c1])
    a2, b2, c2 = exchange(a, "a", 1), exchange(b, "b", 1), exchange(c01, "z", 1)
    s01 = core_swap(c01)
    a, b = jnp.concatenate([a, a2]), jnp.concatenate([b, b2])
    a3, b3, c3 = exchange(a, "a", 2), exchange(b, "b", 2), exchange(c2, "z", 2)
    s2 = core_swap(c2)
    a, b = jnp.concatenate([a, a3]), jnp.concatenate([b, b3])
    a4, b4, c4 = exchange(a, "a", 3), exchange(b, "b", 3), exchange(c3, "z", 3)
    s3 = core_swap(c3)
    near_starts = jnp.concatenate([a_starts[:8], b_starts[:8]])
    starts1 = jnp.concatenate([own_starts[:4], other_starts[:4]])
    starts2 = jnp.concatenate([own_starts[4:], other_starts[4:]])
    near = tile_max([a, b], near_starts, [c01, c2, s01, s2], starts1)
    s4 = core_swap(c4)
    near = jnp.maximum(near, tile_max([a, b], near_starts, [c3, c4, s3, s4], starts2))
    every, every_starts = [c01, c2, s01, s2, c3, c4, s3, s4], jnp.concatenate([starts1, starts2])
    far_a = tile_max([a4], a_starts[8:], every, every_starts)
    far_b = tile_max([b4], b_starts[8:], every, every_starts)
    near = near.reshape(2, 8, half)
    best_a = jnp.concatenate([near[0], far_a.reshape(8, half)])
    best_b = jnp.concatenate([near[1], far_b.reshape(8, half)])
    best_b = best_b.reshape(2, 2, 2, 2, half).transpose(2, 3, 0, 1, 4).reshape(16, half)
    best = jnp.concatenate([best_a, best_b], axis=1)
    for step in (3, 2, 1, 0):
        kept = best.shape[0] // 2
        best = jnp.maximum(best[:kept], exchange(best[kept:], "a", step))
    return jnp.maximum(best.reshape(rows), jnp.float32(-1.0))


def to_unit(values):
    wide = values.astype(jnp.float32)
    inverse = lax.rsqrt(jnp.sum(wide * wide, axis=-1, keepdims=True) + 1e-06)
    return (wide * inverse).astype(jnp.bfloat16)


def shifted(block, axis, distance):
    devices = range(lax.axis_size(axis))
    route = [((i - distance) % len(devices), i) for i in devices]
    return lax.ppermute(block, axis, route)


def small_part(small_emb, small_ids, send_rows, target_rows):
    small_unit = to_unit(small_emb)
    block_size = small_unit.shape[0]
    outgoing = jnp.take(small_unit, send_rows, axis=0, mode="clip")
    incoming = shifted(outgoing, "pack", 1)
    member_pos = jnp.arange(block_size, dtype=jnp.int32)
    local_scores = jnp.einsum("id,jd->ij", small_unit, small_unit, preferred_element_type=jnp.float32)
    local_allowed = (small_ids[:, None] == small_ids[None, :]) & (member_pos[None, :] < member_pos[:, None])
    local_max = jnp.max(jnp.where(local_allowed, local_scores, jnp.float32(-1.0)), axis=1)
    cross = jnp.einsum("td,id->ti", incoming, small_unit, preferred_element_type=jnp.float32)
    target_ids = jnp.take(small_ids, target_rows, mode="clip")
    cross = jnp.where(target_ids[:, None] == small_ids[None, :], cross, jnp.float32(-1.0))
    toward_max = jnp.max(cross, axis=0)
    back_max = jnp.max(cross, axis=1)
    returned = shifted(back_max, "pack", -1)
    hits = send_rows[:, None] == member_pos[None, :]
    returned_max = jnp.max(jnp.where(hits, returned[:, None], jnp.float32(-1.0)), axis=0)
    return jnp.maximum(jnp.maximum(local_max, toward_max), returned_max)


def body(giant_emb, small_emb, small_ids, send_rows, target_rows):
    return giant_part(giant_emb), small_part(small_emb, small_ids, send_rows, target_rows)


def solution(mesh):
    spread = P(AXES)
    wide = P(AXES, None)
    return jax.shard_map(
        body,
        mesh=mesh,
        in_specs=(wide, wide, spread, spread, spread),
        out_specs=(spread, spread),
        check_vma=False,
    )
```

time: 176 us -> 92.9 us (0.53)
  the two profiles are of different devices: /device:TPU:1 before, /device:TPU:6 now
where the time goes in v1:
time: 92.9 us; the launch traced here: 92.3 us
  starting transfers between devices  27.7 us (30%)
  waiting for transfers between devices  20.9 us (22%)
  Pallas kernels  16 us (17%)
  local copies, waits for them, and re-layouts  12.6 us (14%)
  other arithmetic  7.78 us (8%)
  matrix products  5.09 us (5%)
  between operations  2.14 us (2%)
    ppermute x16, starting transfers between devices, exchange(): return lax.ppermute(block, AXES, route)  25.1 us
    ppermute x16, waiting for transfers between devices, exchange(): return lax.ppermute(block, AXES, route)  19.4 us
    pallas_call x4, Pallas kernels, tile_max(): pl.pallas_call(functools.partial(tile_kernel, len(r_list), len(c_list)),...  15.9 us
    unnamed x26, local copies, waits for them, and re-layouts  6.73 us
    gather x1, local copies, waits for them, and re-layouts, small_part(): outgoing = jnp.take(small_unit, send_rows, axis=0, mode='clip')  3.61 us
    dot_general x1, matrix products, small_part(): jnp.einsum('td,id->ti', incoming, small_unit, preferred_element_type=jnp....  2.6 us
    dot_general x1, matrix products, small_part(): jnp.einsum('id,jd->ij', small_unit, small_unit, preferred_element_type=jn...  2.49 us
    concatenate x2, other arithmetic, giant_part(): a, b = (jnp.concatenate([a, a3]), jnp.concatenate([b, b3]))  2.39 us
  transfers between devices with their start and end apart: 22, of which 8 were waited for; matrix products, arithmetic and copies ran while one was open for 20% of the time, Pallas kernels for 17%

profile of v1, /device:TPU:6, one launch (start us, length us, event | category | flops | bytes accessed | tf_op | source)
XLA Modules:
  0.0 92.3 jit_solution(16101602596774689831)
XLA Ops:
  1.7 2.0 %collective-permute-start.6 = (bf16[128,1024]{1,0:T(8,128)(2,1)S(1)}, bf16[128,1024]{1,0:T(8,128)(2,1)S(1)}, u32[]{:S(2)}, u32[]{:S(2)}) collective-permute-start(bf16[128,1024]{1,0:T(8,128)(2,1)S(1)} %shard_map.68), channel_id=1, source_target_pairs={{0,1},{4,39},{1,0},{5,6},{2,3},{6,5},{3,2},{7,36},{32,33},{36,7},{... | collective-permute-start | bytes 786440 | tf_op jit(solution)/shard_map/ppermute | solution.py:49
  5.8 2.1 %fusion = f32[1024]{0:T(1024)S(1)} fusion(bf16[1024,1024]{1,0:T(8,128)(2,1)} %param.6), kind=kLoop, calls=%fused_computation.4 | loop fusion | flops 3144704 | bytes 2101248 | tf_op jit(solution)/shard_map/reduce_sum | solution.py:184
  8.8 1.7 %collective-permute-start.1 = (bf16[128,1024]{1,0:T(8,128)(2,1)S(1)}, bf16[128,1024]{1,0:T(8,128)(2,1)S(1)}, u32[]{:S(2)}, u32[]{:S(2)}) collective-permute-start(bf16[128,1024]{1,0:T(8,128)(2,1)S(1)} %pad_maximum_fusion.5), channel_id=1, source_target_pairs={{0,64},{4,12},{1,65},{5,13},{2,66},{6,14},{3,67},{7,15},{32,96},{3... | collective-permute-start | bytes 786440 | tf_op jit(solution)/shard_map/ppermute | solution.py:49
  10.6 5.0 %collective-permute-start.7 = (bf16[256,1024]{1,0:T(8,128)(2,1)S(1)}, bf16[256,1024]{1,0:T(8,128)(2,1)S(1)}, u32[]{:S(2)}, u32[]{:S(2)}) collective-permute-start(bf16[256,1024]{1,0:T(8,128)(2,1)S(1)} %pad_maximum_fusion.4.refs_2_.refs_1_), channel_id=1, source_target_pairs={{0,35},{4,5},{1,2},{5,4},{2,1},{6,7},{3,32},{7,6},{32,3},{36,37},{... | collective-permute-start | bytes 1572872 | tf_op jit(solution)/shard_map/ppermute | solution.py:49
  16.1 2.3 %collective-permute-start.4 = (bf16[128,1024]{1,0:T(8,128)(2,1)S(1)}, bf16[128,1024]{1,0:T(8,128)(2,1)S(1)}, u32[]{:S(2)}, u32[]{:S(2)}) collective-permute-start(bf16[128,1024]{1,0:T(8,128)(2,1)S(1)} %pad_maximum_fusion.6), channel_id=1, source_target_pairs={{0,192},{4,28},{1,193},{5,29},{2,194},{6,30},{3,195},{7,31},{32,22... | collective-permute-start | bytes 786440 | tf_op jit(solution)/shard_map/ppermute | solution.py:49
  19.6 3.1 %collective-permute-done.7.refs_3_.refs_2_ = bf16[256,1024]{1,0:T(8,128)(2,1)S(1)} collective-permute-done((bf16[256,1024]{1,0:T(8,128)(2,1)S(1)}, bf16[256,1024]{1,0:T(8,128)(2,1)S(1)}, u32[]{:S(2)}, u32[]{:S(2)}) %collective-permute-start.7) | collective-permute-done | bytes 524320 | tf_op jit(solution)/shard_map/ppermute | solution.py:49
  22.8 2.5 %select_reduce_fusion = f32[1024]{0:T(1024)S(1)} fusion(s32[1024]{0:T(1024)S(1)} %copy-done.7, bf16[1024,1024]{1,0:T(8,128)(2,1)S(1)} %fusion.1), kind=kOutput, calls=%fused_computation.6 | convolution fusion | flops 2152725504 | bytes 2105344 | tf_op jit(solution)/shard_map/id,jd->ij/dot_general | solution.py:200
  26.4 5.6 %collective-permute-done.10.refs_2_.refs_5_ = bf16[256,1024]{1,0:T(8,128)(2,1)} collective-permute-done((bf16[256,1024]{1,0:T(8,128)(2,1)S(1)}, bf16[256,1024]{1,0:T(8,128)(2,1)}, u32[]{:S(2)}, u32[]{:S(2)}) %collective-permute-start.10) | collective-permute-done | bytes 524320 | tf_op jit(solution)/shard_map/ppermute | solution.py:49
  32.0 3.8 %collective-permute-start.11 = (bf16[256,1024]{1,0:T(8,128)(2,1)}, bf16[256,1024]{1,0:T(8,128)(2,1)}, u32[]{:S(2)}, u32[]{:S(2)}) collective-permute-start(bf16[256,1024]{1,0:T(8,128)(2,1)} %collective-permute-done.10.refs_2_.refs_5_), channel_id=1, source_target_pairs={{0,35},{4,5},{1,2},{5,4},{2,1},{6,7},{3,32},{7,6},{32,3},{36,37},{... | collective-permute-start | bytes 1572872 | tf_op jit(solution)/shard_map/ppermute | solution.py:49
  37.0 1.7 %collective-permute-start.14 = (bf16[512,1024]{1,0:T(8,128)(2,1)S(1)}, bf16[512,1024]{1,0:T(8,128)(2,1)}, u32[]{:S(2)}, u32[]{:S(2)}) collective-permute-start(bf16[512,1024]{1,0:T(8,128)(2,1)S(1)} %pad_maximum_fusion.refs_0_), channel_id=1, source_target_pairs={{0,192},{4,28},{1,193},{5,29},{2,194},{6,30},{3,195},{7,31},{32,22... | collective-permute-start | bytes 3145736 | tf_op jit(solution)/shard_map/ppermute | solution.py:49
  40.2 3.6 %gather_fusion.1 = bf16[128,1024]{1,0:T(8,128)(2,1)} fusion(bf16[1024,1024]{1,0:T(8,128)(2,1)} %copy-done.8, s32[1024]{0:T(1024)S(1)} %pad_clamp_fusion), kind=kCustom, calls=%fused_computation.1 | custom fusion | bytes 524800 | tf_op jit(solution)/shard_map/jit(_take)/gather | solution.py:197
  46.8 3.7 %shard_map.69 = f32[1,1024]{1,0:T(1,128)S(1)} custom-call(s32[16]{0:T(128)S(1)} %pad_add_fusion.r_starts, s32[8]{0:T(128)S(1)} %concatenate.55.c_starts, bf16[512,1024]{1,0:T(8,128)(2,1)S(1)} %pad_maximum_fusion.refs_0_, bf16[512,1024]{1,0:T(8,128)(2,1)S(1)} %pad_maximum_fusion.1.refs_1_, bf16[256,1024]{1,0:T(8,128)(2,1)S(1)} %pad_maximum_fusion.4.refs_2_.refs_1_, ...), custom_call_target="tpu_custom_call" | custom-call | flops 2147483648 | bytes 4194304 | tf_op jit(solution)/shard_map/pallas_call | solution.py:104
  50.4 2.7 %collective-permute-done.14.refs_0_ = bf16[512,1024]{1,0:T(8,128)(2,1)} collective-permute-done((bf16[512,1024]{1,0:T(8,128)(2,1)S(1)}, bf16[512,1024]{1,0:T(8,128)(2,1)}, u32[]{:S(2)}, u32[]{:S(2)}) %collective-permute-start.14) | collective-permute-done | bytes 1048608 | tf_op jit(solution)/shard_map/ppermute | solution.py:49
  53.2 4.3 %shard_map.71 = f32[1,512]{1,0:T(1,128)S(1)} custom-call(s32[8]{0:T(128)S(1)} %get-tuple-element.8.r_starts, s32[16]{0:T(128)S(1)} %concatenate.64.c_starts, bf16[512,1024]{1,0:T(8,128)(2,1)} %collective-permute-done.14.refs_0_, bf16[256,1024]{1,0:T(8,128)(2,1)S(1)} %pad_maximum_fusion.4.refs_2_.refs_1_, ...), custom_call_target="tpu_custom_call" | custom-call | flops 2147483648 | bytes 5242880 | tf_op jit(solution)/shard_map/pallas_call | solution.py:104
  62.4 3.7 %shard_map.70 = f32[1,1024]{1,0:T(1,128)S(1)} custom-call(s32[16]{0:T(128)S(1)} %pad_add_fusion.r_starts, s32[8]{0:T(128)S(1)} %concatenate.63.c_starts, bf16[512,1024]{1,0:T(8,128)(2,1)S(1)} %pad_maximum_fusion.refs_0_, bf16[512,1024]{1,0:T(8,128)(2,1)S(1)} %pad_maximum_fusion.1.refs_1_, bf16[256,1024]{1,0:T(8,128)(2,1)} %collective-permute-done.10.refs_2_.refs_5_, ...), custom_call_target="tpu_custom_call" | custom-call | flops 2147483648 | bytes 4194304 | tf_op jit(solution)/shard_map/pallas_call | solution.py:104
  68.3 4.3 %shard_map.72 = f32[1,512]{1,0:T(1,128)S(1)} custom-call(s32[8]{0:T(128)S(1)} %get-tuple-element.11.r_starts, s32[16]{0:T(128)S(1)} %concatenate.64.c_starts, bf16[512,1024]{1,0:T(8,128)(2,1)} %collective-permute-done.15.refs_0_, bf16[256,1024]{1,0:T(8,128)(2,1)S(1)} %pad_maximum_fusion.4.refs_2_.refs_1_, ...), custom_call_target="tpu_custom_call" | custom-call | flops 2147483648 | bytes 5242880 | tf_op jit(solution)/shard_map/pallas_call | solution.py:104
  73.5 1.7 %collective-permute-start.16 = (f32[8,128]{1,0:T(8,128)S(1)}, f32[8,128]{1,0:T(8,128)S(1)}, u32[]{:S(2)}, u32[]{:S(2)}) collective-permute-start(f32[8,128]{1,0:T(8,128)S(1)} %slice.83), channel_id=1, source_target_pairs={{0,192},{4,28},{1,193},{5,29},{2,194},{6,30},{3,195},{7,31},{32,22... | collective-permute-start | bytes 12296 | tf_op jit(solution)/shard_map/ppermute | solution.py:49
  76.2 2.2 %collective-permute-done.16 = f32[8,128]{1,0:T(8,128)S(1)} collective-permute-done((f32[8,128]{1,0:T(8,128)S(1)}, f32[8,128]{1,0:T(8,128)S(1)}, u32[]{:S(2)}, u32[]{:S(2)}) %collective-permute-start.16) | collective-permute-done | bytes 4128 | tf_op jit(solution)/shard_map/ppermute | solution.py:49
  78.4 1.6 %collective-permute-start.17 = (f32[4,128]{1,0:T(4,128)S(1)}, f32[4,128]{1,0:T(4,128)S(1)}, u32[]{:S(2)}, u32[]{:S(2)}) collective-permute-start(f32[4,128]{1,0:T(4,128)S(1)} %slice.69), channel_id=1, source_target_pairs={{0,24},{4,196},{1,25},{5,197},{2,26},{6,198},{3,27},{7,199},{32,56... | collective-permute-start | bytes 6152 | tf_op jit(solution)/shard_map/ppermute | solution.py:49
  80.0 2.6 %fusion.4 = (f32[1024]{0:T(1024)S(1)}, f32[128]{0:T(128)S(1)}) fusion(bf16[128,1024]{1,0:T(8,128)(2,1)} %collective-permute-done.20, bf16[1024,1024]{1,0:T(8,128)(2,1)} %copy-done.8, s32[1024]{0:T(1024)S(1)} %copy-done.7, s32[128]{0:T(128)S(1)} %gather_fusion), kind=kOutput, calls=%fused_computation.39 | convolution fusion | flops 268958592 | bytes 2368512 | tf_op jit(solution)/shard_map/td,id->ti/dot_general | solution.py:203
  82.6 2.0 %collective-permute-start.21 = (f32[128]{0:T(128)S(1)}, f32[128]{0:T(128)S(1)}, u32[]{:S(2)}, u32[]{:S(2)}) collective-permute-start(f32[128]{0:T(128)S(1)} %get-tuple-element.3), channel_id=1, source_target_pairs={{1,0},{2,1},{3,2},{0,3},{5,4},{6,5},{7,6},{4,7},{9,8},{10,9},{11,1... | collective-permute-start | bytes 1544 | tf_op jit(solution)/shard_map/ppermute | solution.py:191
  84.7 1.5 %collective-permute-done.21 = f32[128]{0:T(128)S(1)} collective-permute-done((f32[128]{0:T(128)S(1)}, f32[128]{0:T(128)S(1)}, u32[]{:S(2)}, u32[]{:S(2)}) %collective-permute-start.21) | collective-permute-done | bytes 544 | tf_op jit(solution)/shard_map/ppermute | solution.py:191
  86.3 1.9 %collective-permute-done.18 = f32[2,128]{1,0:T(2,128)S(1)} collective-permute-done((f32[2,128]{1,0:T(2,128)S(1)}, f32[2,128]{1,0:T(2,128)S(1)}, u32[]{:S(2)}, u32[]{:S(2)}) %collective-permute-start.18) | collective-permute-done | bytes 1056 | tf_op jit(solution)/shard_map/ppermute | solution.py:49
  88.9 2.9 %collective-permute-done.19 = f32[1,128]{1,0:T(1,128)S(1)} collective-permute-done((f32[1,128]{1,0:T(1,128)S(1)}, f32[1,128]{1,0:T(1,128)S(1)}, u32[]{:S(2)}, u32[]{:S(2)}) %collective-permute-start.19) | collective-permute-done | bytes 544 | tf_op jit(solution)/shard_map/ppermute | solution.py:49
  (97 shorter events, 21.8 us)
Async XLA Ops:
  1.7 13.9 %copy-start.9 = (bf16[1024,1024]{1,0:T(8,128)(2,1)S(1)}, bf16[1024,1024]{1,0:T(8,128)(2,1)}, u32[]{:S(2)}) copy-start(bf16[1024,1024]{1,0:T(8,128)(2,1)} %param.6) | copy-start | bytes 6291460
  1.7 8.8 %collective-permute-start.6 = (bf16[128,1024]{1,0:T(8,128)(2,1)S(1)}, bf16[128,1024]{1,0:T(8,128)(2,1)S(1)}, u32[]{:S(2)}, u32[]{:S(2)}) collective-permute-start(bf16[128,1024]{1,0:T(8,128)(2,1)S(1)} %shard_map.68), channel_id=1, source_target_pairs={{0,1},{4,39},{1,0},{5,6},{2,3},{6,5},{3,2},{7,36},{32,33},{36,7},{... | collective-permute-start | bytes 786440 | tf_op jit(solution)/shard_map/ppermute | solution.py:49
  3.8 5.1 %collective-permute-start = (bf16[64,1024]{1,0:T(8,128)(2,1)S(1)}, bf16[64,1024]{1,0:T(8,128)(2,1)S(1)}, u32[]{:S(2)}, u32[]{:S(2)}) collective-permute-start(bf16[64,1024]{1,0:T(8,128)(2,1)S(1)} %get-tuple-element.6), channel_id=1, source_target_pairs={{0,8},{4,68},{1,9},{5,69},{2,10},{6,70},{3,11},{7,71},{32,40},{36,... | collective-permute-start | bytes 393224 | tf_op jit(solution)/shard_map/ppermute | solution.py:49
  4.7 11.3 %collective-permute-start.3 = (bf16[64,1024]{1,0:T(8,128)(2,1)S(1)}, bf16[64,1024]{1,0:T(8,128)(2,1)S(1)}, u32[]{:S(2)}, u32[]{:S(2)}) collective-permute-start(bf16[64,1024]{1,0:T(8,128)(2,1)S(1)} %get-tuple-element.7), channel_id=1, source_target_pairs={{0,24},{4,196},{1,25},{5,197},{2,26},{6,198},{3,27},{7,199},{32,56... | collective-permute-start | bytes 393224 | tf_op jit(solution)/shard_map/ppermute | solution.py:49
  8.8 9.5 %collective-permute-start.1 = (bf16[128,1024]{1,0:T(8,128)(2,1)S(1)}, bf16[128,1024]{1,0:T(8,128)(2,1)S(1)}, u32[]{:S(2)}, u32[]{:S(2)}) collective-permute-start(bf16[128,1024]{1,0:T(8,128)(2,1)S(1)} %pad_maximum_fusion.5), channel_id=1, source_target_pairs={{0,64},{4,12},{1,65},{5,13},{2,66},{6,14},{3,67},{7,15},{32,96},{3... | collective-permute-start | bytes 786440 | tf_op jit(solution)/shard_map/ppermute | solution.py:49
  10.6 12.2 %collective-permute-start.7 = (bf16[256,1024]{1,0:T(8,128)(2,1)S(1)}, bf16[256,1024]{1,0:T(8,128)(2,1)S(1)}, u32[]{:S(2)}, u32[]{:S(2)}) collective-permute-start(bf16[256,1024]{1,0:T(8,128)(2,1)S(1)} %pad_maximum_fusion.4.refs_2_.refs_1_), channel_id=1, source_target_pairs={{0,35},{4,5},{1,2},{5,4},{2,1},{6,7},{3,32},{7,6},{32,3},{36,37},{... | collective-permute-start | bytes 1572872 | tf_op jit(solution)/shard_map/ppermute | solution.py:49
  16.1 9.3 %collective-permute-start.4 = (bf16[128,1024]{1,0:T(8,128)(2,1)S(1)}, bf16[128,1024]{1,0:T(8,128)(2,1)S(1)}, u32[]{:S(2)}, u32[]{:S(2)}) collective-permute-start(bf16[128,1024]{1,0:T(8,128)(2,1)S(1)} %pad_maximum_fusion.6), channel_id=1, source_target_pairs={{0,192},{4,28},{1,193},{5,29},{2,194},{6,30},{3,195},{7,31},{32,22... | collective-permute-start | bytes 786440 | tf_op jit(solution)/shard_map/ppermute | solution.py:49
  18.4 17.4 %collective-permute-start.2 = (bf16[256,1024]{1,0:T(8,128)(2,1)S(1)}, bf16[256,1024]{1,0:T(8,128)(2,1)}, u32[]{:S(2)}, u32[]{:S(2)}) collective-permute-start(bf16[256,1024]{1,0:T(8,128)(2,1)S(1)} %pad_maximum_fusion.2), channel_id=1, source_target_pairs={{0,24},{4,196},{1,25},{5,197},{2,26},{6,198},{3,27},{7,199},{32,56... | collective-permute-start | bytes 1572872 | tf_op jit(solution)/shard_map/ppermute | solution.py:49
  22.7 9.3 %collective-permute-start.10 = (bf16[256,1024]{1,0:T(8,128)(2,1)S(1)}, bf16[256,1024]{1,0:T(8,128)(2,1)}, u32[]{:S(2)}, u32[]{:S(2)}) collective-permute-start(bf16[256,1024]{1,0:T(8,128)(2,1)S(1)} %collective-permute-done.7.refs_3_.refs_2_), channel_id=1, source_target_pairs={{0,1},{4,39},{1,0},{5,6},{2,3},{6,5},{3,2},{7,36},{32,33},{36,7},{... | collective-permute-start | bytes 1572872 | tf_op jit(solution)/shard_map/ppermute | solution.py:49
  25.3 13.5 %copy-start.11 = (s32[128]{0:T(128)S(1)}, s32[128]{0:T(128)}, u32[]{:S(2)}) copy-start(s32[128]{0:T(128)} %param.8) | copy-start | bytes 1540
  25.4 18.4 %collective-permute-start.5 = (bf16[256,1024]{1,0:T(8,128)(2,1)S(1)}, bf16[256,1024]{1,0:T(8,128)(2,1)}, u32[]{:S(2)}, u32[]{:S(2)}) collective-permute-start(bf16[256,1024]{1,0:T(8,128)(2,1)S(1)} %pad_maximum_fusion.3), channel_id=1, source_target_pairs={{0,8},{4,68},{1,9},{5,69},{2,10},{6,70},{3,11},{7,71},{32,40},{36,... | collective-permute-start | bytes 1572872 | tf_op jit(solution)/shard_map/ppermute | solution.py:49
  26.3 19.7 %collective-permute-start.8 = (bf16[256,1024]{1,0:T(8,128)(2,1)S(1)}, bf16[256,1024]{1,0:T(8,128)(2,1)}, u32[]{:S(2)}, u32[]{:S(2)}) collective-permute-start(bf16[256,1024]{1,0:T(8,128)(2,1)S(1)} %pad_maximum_fusion.4.refs_2_.refs_1_), channel_id=1, source_target_pairs={{0,4},{4,0},{1,5},{5,1},{2,6},{6,2},{3,7},{7,3},{32,36},{36,32},{3... | collective-permute-start | bytes 1572872 | tf_op jit(solution)/shard_map/ppermute | solution.py:57
  32.0 14.2 %collective-permute-start.11 = (bf16[256,1024]{1,0:T(8,128)(2,1)}, bf16[256,1024]{1,0:T(8,128)(2,1)}, u32[]{:S(2)}, u32[]{:S(2)}) collective-permute-start(bf16[256,1024]{1,0:T(8,128)(2,1)} %collective-permute-done.10.refs_2_.refs_5_), channel_id=1, source_target_pairs={{0,35},{4,5},{1,2},{5,4},{2,1},{6,7},{3,32},{7,6},{32,3},{36,37},{... | collective-permute-start | bytes 1572872 | tf_op jit(solution)/shard_map/ppermute | solution.py:49
  37.0 16.2 %collective-permute-start.14 = (bf16[512,1024]{1,0:T(8,128)(2,1)S(1)}, bf16[512,1024]{1,0:T(8,128)(2,1)}, u32[]{:S(2)}, u32[]{:S(2)}) collective-permute-start(bf16[512,1024]{1,0:T(8,128)(2,1)S(1)} %pad_maximum_fusion.refs_0_), channel_id=1, source_target_pairs={{0,192},{4,28},{1,193},{5,29},{2,194},{6,30},{3,195},{7,31},{32,22... | collective-permute-start | bytes 3145736 | tf_op jit(solution)/shard_map/ppermute | solution.py:49
  38.8 8.0 %collective-permute-start.9 = (bf16[256,1024]{1,0:T(8,128)(2,1)S(1)}, bf16[256,1024]{1,0:T(8,128)(2,1)}, u32[]{:S(2)}, u32[]{:S(2)}) collective-permute-start(bf16[256,1024]{1,0:T(8,128)(2,1)S(1)} %collective-permute-done.7.refs_3_.refs_2_), channel_id=1, source_target_pairs={{0,4},{4,0},{1,5},{5,1},{2,6},{6,2},{3,7},{7,3},{32,36},{36,32},{3... | collective-permute-start | bytes 1572872 | tf_op jit(solution)/shard_map/ppermute | solution.py:57
  45.1 21.1 %collective-permute-start.15 = (bf16[512,1024]{1,0:T(8,128)(2,1)S(1)}, bf16[512,1024]{1,0:T(8,128)(2,1)}, u32[]{:S(2)}, u32[]{:S(2)}) collective-permute-start(bf16[512,1024]{1,0:T(8,128)(2,1)S(1)} %pad_maximum_fusion.1.refs_1_), channel_id=1, source_target_pairs={{0,64},{4,12},{1,65},{5,13},{2,66},{6,14},{3,67},{7,15},{32,96},{3... | collective-permute-start | bytes 3145736 | tf_op jit(solution)/shard_map/ppermute | solution.py:49
  46.1 4.4 %collective-permute-start.12 = (bf16[256,1024]{1,0:T(8,128)(2,1)}, bf16[256,1024]{1,0:T(8,128)(2,1)S(1)}, u32[]{:S(2)}, u32[]{:S(2)}) collective-permute-start(bf16[256,1024]{1,0:T(8,128)(2,1)} %collective-permute-done.10.refs_2_.refs_5_), channel_id=1, source_target_pairs={{0,4},{4,0},{1,5},{5,1},{2,6},{6,2},{3,7},{7,3},{32,36},{36,32},{3... | collective-permute-start | bytes 1572872 | tf_op jit(solution)/shard_map/ppermute | solution.py:57
  46.2 7.0 %collective-permute-start.13 = (bf16[256,1024]{1,0:T(8,128)(2,1)}, bf16[256,1024]{1,0:T(8,128)(2,1)S(1)}, u32[]{:S(2)}, u32[]{:S(2)}) collective-permute-start(bf16[256,1024]{1,0:T(8,128)(2,1)} %collective-permute-done.11.refs_3_.refs_6_), channel_id=1, source_target_pairs={{0,4},{4,0},{1,5},{5,1},{2,6},{6,2},{3,7},{7,3},{32,36},{36,32},{3... | collective-permute-start | bytes 1572872 | tf_op jit(solution)/shard_map/ppermute | solution.py:57
  46.7 33.3 %collective-permute-start.20 = (bf16[128,1024]{1,0:T(8,128)(2,1)}, bf16[128,1024]{1,0:T(8,128)(2,1)}, u32[]{:S(2)}, u32[]{:S(2)}) collective-permute-start(bf16[128,1024]{1,0:T(8,128)(2,1)} %gather_fusion.1), channel_id=1, source_target_pairs={{3,0},{0,1},{1,2},{2,3},{7,4},{4,5},{5,6},{6,7},{11,8},{8,9},{9,10... | collective-permute-start | bytes 786440 | tf_op jit(solution)/shard_map/ppermute | solution.py:191
  73.5 4.8 %collective-permute-start.16 = (f32[8,128]{1,0:T(8,128)S(1)}, f32[8,128]{1,0:T(8,128)S(1)}, u32[]{:S(2)}, u32[]{:S(2)}) collective-permute-start(f32[8,128]{1,0:T(8,128)S(1)} %slice.83), channel_id=1, source_target_pairs={{0,192},{4,28},{1,193},{5,29},{2,194},{6,30},{3,195},{7,31},{32,22... | collective-permute-start | bytes 12296 | tf_op jit(solution)/shard_map/ppermute | solution.py:49
  78.4 6.2 %collective-permute-start.17 = (f32[4,128]{1,0:T(4,128)S(1)}, f32[4,128]{1,0:T(4,128)S(1)}, u32[]{:S(2)}, u32[]{:S(2)}) collective-permute-start(f32[4,128]{1,0:T(4,128)S(1)} %slice.69), channel_id=1, source_target_pairs={{0,24},{4,196},{1,25},{5,197},{2,26},{6,198},{3,27},{7,199},{32,56... | collective-permute-start | bytes 6152 | tf_op jit(solution)/shard_map/ppermute | solution.py:49
  82.6 3.6 %collective-permute-start.21 = (f32[128]{0:T(128)S(1)}, f32[128]{0:T(128)S(1)}, u32[]{:S(2)}, u32[]{:S(2)}) collective-permute-start(f32[128]{0:T(128)S(1)} %get-tuple-element.3), channel_id=1, source_target_pairs={{1,0},{2,1},{3,2},{0,3},{5,4},{6,5},{7,6},{4,7},{9,8},{10,9},{11,1... | collective-permute-start | bytes 1544 | tf_op jit(solution)/shard_map/ppermute | solution.py:191
  84.6 3.7 %collective-permute-start.18 = (f32[2,128]{1,0:T(2,128)S(1)}, f32[2,128]{1,0:T(2,128)S(1)}, u32[]{:S(2)}, u32[]{:S(2)}) collective-permute-start(f32[2,128]{1,0:T(2,128)S(1)} %slice.71), channel_id=1, source_target_pairs={{0,64},{4,12},{1,65},{5,13},{2,66},{6,14},{3,67},{7,15},{32,96},{3... | collective-permute-start | bytes 3080 | tf_op jit(solution)/shard_map/ppermute | solution.py:49
  88.3 3.5 %collective-permute-start.19 = (f32[1,128]{1,0:T(1,128)S(1)}, f32[1,128]{1,0:T(1,128)S(1)}, u32[]{:S(2)}, u32[]{:S(2)}) collective-permute-start(f32[1,128]{1,0:T(1,128)S(1)} %slice.73), channel_id=1, source_target_pairs={{0,8},{4,68},{1,9},{5,69},{2,10},{6,70},{3,11},{7,71},{32,40},{36,... | collective-permute-start | bytes 1544 | tf_op jit(solution)/shard_map/ppermute | solution.py:49
  (11 other events, 45.5 us)

commit v2 on v0

v2 whole, which is shorter than its diff:
```python
import functools
import jax
import jax.numpy as jnp
from jax import lax
from jax.experimental import pallas as pl
from jax.experimental.pallas import tpu as pltpu
from jax.sharding import PartitionSpec as P

AXES = ("row", "col", "pack")
LOW = -2.0
NT = (((1,), (1,)), ((), ()))
MIB = 1024 * 1024
SMEM = pl.BlockSpec(memory_space=pltpu.SMEM)
VMEM = pl.BlockSpec(memory_space=pltpu.VMEM)
LATER = pl.BlockSpec(memory_space=pl.ANY)


def place(x, y, z, c):
    return ((y * 2 + z // 4) * 8 + x * 2 + c) * 4 + z % 4


def z_step(z, odd):
    return (z + 1 + 6 * ((z + odd) % 2)) % 8


def partner(link, x, y, z, c):
    if link in ("E", "O"):
        return x, y, z_step(z, (link == "O") != (c == 1))
    flip = 1 if link[0] == "P" else 3
    along_x = (len(link) == 1) == (c == 0)
    return (x ^ flip, y, z) if along_x else (x, y ^ flip, z)


def route(move):
    cells = [(x, y, z, c) for x in range(4) for y in range(4) for z in range(8) for c in range(2)]
    return [(place(*cell), place(*move(*cell))) for cell in cells]


def over(block, link):
    return lax.ppermute(block, AXES, route(lambda x, y, z, c: (*partner(link, x, y, z, c), c)))


def core_swap(block):
    return lax.ppermute(block, AXES, route(lambda x, y, z, c: (x, y, z, 1 - c)))


def call(kernel, out_shape, specs, operands, after=(), flops=0, size=0):
    n = len(operands)

    def run(*refs):
        kernel(*refs[:n], *refs[n + len(after) :])

    many = isinstance(out_shape, (tuple, list))
    return pl.pallas_call(
        run,
        out_shape=out_shape,
        in_specs=list(specs) + [LATER] * len(after),
        out_specs=[VMEM] * len(out_shape) if many else VMEM,
        compiler_params=pltpu.CompilerParams(vmem_limit_bytes=8 * MIB),
        cost_estimate=pl.CostEstimate(flops=flops, bytes_accessed=size, transcendentals=0),
    )(*operands, *after)


def shape(rows, columns, dtype):
    return jax.ShapeDtypeStruct((rows, columns), dtype)


def dot_nt(left, right):
    total = None
    for k in range(0, 1024, 256):
        part = lax.dot_general(left[:, k : k + 256], right[:, k : k + 256], NT, preferred_element_type=jnp.float32)
        total = part if total is None else total + part
    return total


def unit_rows(values):
    wide = values.astype(jnp.float32)
    inverse = lax.rsqrt(jnp.sum(wide * wide, axis=-1, keepdims=True) + 1e-06)
    return (wide * inverse).astype(jnp.bfloat16)


def unit_kernel(values, out):
    for i in range(0, values.shape[0], 128):
        out[i : i + 128, :] = unit_rows(values[i : i + 128, :])


def join_kernel(first, second, out):
    rows = first.shape[0]
    out[:rows, :] = first[...]
    out[rows:, :] = second[...]


def join(first, second, after=()):
    rows = first.shape[0] + second.shape[0]
    return call(join_kernel, shape(rows, 1024, jnp.bfloat16), [VMEM] * 2, [first, second], after, size=rows * 4096)


def here():
    row_index, col_index, z_low = (lax.axis_index(a) for a in AXES)
    return col_index >> 1, row_index >> 1, ((row_index & 1) << 2) | z_low, col_index & 1


def first_row(x, y, z, c):
    return ((((((y << 1) | (z >> 2)) << 3) | (x << 1) | c) << 2) | (z & 3)) << 7


def plane_start(at, far, near):
    x, y, z, core = at
    flip = (0, 1, 3, 2)
    if far == near:
        along_x = along_y = flip[far]
    else:
        along_x = jnp.where(core == 0, flip[near], flip[far])
        along_y = jnp.where(core == 0, flip[far], flip[near])
    return first_row(x ^ along_x, y ^ along_y, z, core)


def line_start(at, steps, other):
    x, y, z, core = at
    core = (1 - core) if other else core
    way = 1 - 2 * ((z + core) & 1)
    return first_row(x, y, (z + way * steps + 8) & 7, core)


def tile_kernel(row_names, col_names, n_before, spots, *refs):
    at = here()
    n_r, n_c = len(row_names), len(col_names)
    r_refs, c_refs = refs[:n_r], refs[n_r : n_r + n_c]
    before, outs = refs[n_r + n_c : n_r + n_c + n_before], refs[n_r + n_c + n_before :]
    out_rows = outs[0].shape[0]
    lane = lax.broadcasted_iota(jnp.int32, (1, 256), 1)
    sub = lax.broadcasted_iota(jnp.int32, (128, 256), 0)
    starts = [[line_start(at, name + h if name >= 0 else name - h, other) for h in range(2)] for name, other in col_names]
    for j, (r_ref, (far, near)) in enumerate(zip(r_refs, row_names)):
        row_pos = jnp.where(lane < 128, plane_start(at, far, near) + lane, plane_start(at, far, near + 1) + lane - 128)
        best = jnp.full((8, 256), LOW, jnp.float32)
        for i in range(n_c):
            scores = dot_nt(c_refs[i], r_ref)
            for h in range(2):
                kept = jnp.where(sub < row_pos - starts[i][h], scores[128 * h : 128 * (h + 1)], LOW)
                best = jnp.maximum(best, jnp.max(kept.reshape(16, 8, 256), axis=0))
        best = jnp.max(best, axis=0, keepdims=True)
        for h in range(2):
            spot = 2 * j + h
            value = best[:, 128 * h : 128 * (h + 1)]
            seen = 0
            for b in before:
                if seen <= spot < seen + b.shape[0]:
                    value = jnp.maximum(value, b[spot - seen : spot - seen + 1, :])
                seen += b.shape[0]
            spot = 2 * spots[j] + h
            outs[spot // out_rows][spot % out_rows : spot % out_rows + 1, :] = value


def tile(rows, cols, before=(), after=(), spots=None):
    n = 2 * len(rows)
    out = shape(n, 128, jnp.float32) if spots is None else [shape(n // 2, 128, jnp.float32)] * 2
    operands = [*rows.values(), *cols.values(), *before]
    return call(
        functools.partial(tile_kernel, list(rows), list(cols), len(before), spots or range(len(rows))),
        out, [VMEM] * len(operands), operands, after,
        flops=2 * n * 128 * len(cols) * 256 * 1024, size=(n + 2 * len(cols)) * 256 * 1024,
    )


def fold_kernel(mine, theirs, *outs):
    best = jnp.maximum(mine[...], theirs[...])
    if len(outs) == 1:
        outs[0][...] = jnp.maximum(best, -1.0)
    else:
        half = best.shape[0] // 2
        outs[0][...] = best[:half]
        outs[1][...] = best[half:]


def fold(mine, theirs):
    half = mine.shape[0] // 2
    out = [shape(half, 128, jnp.float32)] * 2 if half else shape(1, 128, jnp.float32)
    return call(fold_kernel, out, [VMEM] * 2, [mine, theirs])


def column(row):
    return jnp.broadcast_to(row, (128, 128)).T


def gather_kernel(unit, send, out):
    lane = lax.broadcasted_iota(jnp.int32, (128, 128), 1)
    wanted = column(send[...])
    total = None
    for k in range(0, 1024, 256):
        hit = jnp.concatenate([wanted == lane + k, wanted == lane + k + 128], axis=1)
        part = jnp.dot(hit.astype(jnp.bfloat16), unit[k : k + 256, :], preferred_element_type=jnp.float32)
        total = part if total is None else total + part
    out[...] = total.astype(jnp.bfloat16)


def local_kernel(unit, ids, out):
    sub = lax.broadcasted_iota(jnp.int32, (256, 256), 0)
    lane = lax.broadcasted_iota(jnp.int32, (256, 256), 1)
    id_col = []
    for j in range(4):
        parts = [column(ids[:, 256 * j + 128 * h : 256 * j + 128 * (h + 1)]) for h in range(2)]
        part = jnp.concatenate(parts)
        id_col.append(jnp.concatenate([part, part], axis=1))
    for i in range(4):
        rows = slice(256 * i, 256 * (i + 1))
        best = jnp.full((8, 256), -1.0, jnp.float32)
        for j in range(i + 1):
            scores = dot_nt(unit[256 * j : 256 * (j + 1), :], unit[rows, :])
            allowed = id_col[j] == ids[:, rows]
            if i == j:
                allowed = allowed & (sub < lane)
            scores = jnp.where(allowed, scores, -1.0)
            best = jnp.maximum(best, jnp.max(scores.reshape(32, 8, 256), axis=0))
        out[:, rows] = jnp.max(best, axis=0, keepdims=True)


def cross_kernel(incoming, unit, ids, target, toward, back):
    lane = lax.broadcasted_iota(jnp.int32, (128, 128), 1)
    wanted = column(target[...])
    found = jnp.zeros((128, 128), jnp.int32)
    for k in range(0, 1024, 128):
        found = found + jnp.where(wanted == lane + k, ids[:, k : k + 128], 0)
    target_id = jnp.sum(found, axis=1, keepdims=True)
    back_best = jnp.full((128, 128), -1.0, jnp.float32)
    for i in range(0, 1024, 256):
        scores = dot_nt(incoming[...], unit[i : i + 256, :])
        scores = jnp.where(target_id == ids[:, i : i + 256], scores, -1.0)
        toward[:, i : i + 256] = jnp.max(scores, axis=0, keepdims=True)
        back_best = jnp.maximum(back_best, jnp.maximum(scores[:, :128], scores[:, 128:]))
    back[...] = jnp.max(back_best.T, axis=0, keepdims=True)


def finish_kernel(returned, send, local, toward, out):
    lane = lax.broadcasted_iota(jnp.int32, (128, 128), 1)
    wanted, value = column(send[...]), column(returned[...])
    for k in range(0, 1024, 128):
        hit = jnp.max(jnp.where(wanted == lane + k, value, -1.0), axis=0, keepdims=True)
        out[:, k : k + 128] = jnp.maximum(jnp.maximum(local[:, k : k + 128], toward[:, k : k + 128]), hit)


def pack_shift(block, distance):
    size = lax.axis_size("pack")
    return lax.ppermute(block, "pack", [((i - distance) % size, i) for i in range(size)])


def body(giant_emb, small_emb, small_ids, send_rows, target_rows):
    ids, send, target = small_ids.reshape(1, 1024), send_rows.reshape(1, 128), target_rows.reshape(1, 128)

    own = call(unit_kernel, shape(128, 1024, jnp.bfloat16), [VMEM], [giant_emb])
    e, p, q = over(own, "E"), over(own, "P"), over(own, "Q")
    small = call(unit_kernel, shape(1024, 1024, jnp.bfloat16), [VMEM], [small_emb], [own], size=4 * MIB)
    c1 = join(own, e, [small])
    c2, d1 = over(c1, "O"), core_swap(c1)
    a = join(own, p, [c1])
    pq = over(p, "Q")
    a_p, a_q = over(a, "P2"), over(a, "Q2")
    local = call(local_kernel, shape(1, 1024, jnp.float32), [VMEM] * 2, [small, ids], [a], flops=20 * 2**26)
    b = join(q, pq, [local])
    b_p, b_q = over(b, "P2"), over(b, "Q2")
    outgoing = call(gather_kernel, shape(128, 1024, jnp.bfloat16), [VMEM] * 2, [small, send], [b], flops=2**28)
    one = tile({(0, 0): a, (0, 2): b}, {(0, False): c1, (0, True): d1}, after=[outgoing])
    a_pq = over(a_p, "Q2")
    c3, d2 = over(c2, "E"), core_swap(c2)
    two = tile(
        {(1, 0): a_p, (2, 0): a_q}, {(0, False): c1, (0, True): d1, (-1, False): c2, (-1, True): d2}, after=[one],
    )
    b_pq = over(b_q, "P2")
    three = tile(
        {(1, 2): b_p, (2, 2): b_q}, {(0, False): c1, (0, True): d1, (-1, False): c2, (-1, True): d2}, after=[two],
    )
    one = tile({(0, 0): a, (0, 2): b}, {(-1, False): c2, (-1, True): d2}, [one], after=[three])
    c4, d3 = over(c3, "O"), core_swap(c3)
    incoming = pack_shift(outgoing, 1)
    four = tile(
        {(3, 0): a_pq, (3, 2): b_pq},
        {(0, False): c1, (0, True): d1, (-1, False): c2, (-1, True): d2, (2, False): c3, (2, True): d3}, after=[one],
    )
    rows = {
        (0, 0): a, (0, 2): b, (1, 0): a_p, (2, 0): a_q, (1, 2): b_p, (2, 2): b_q,
    }
    five = tile(rows, {(2, False): c3, (2, True): d3}, [one, two, three], after=[four])
    d4 = core_swap(c4)
    rows = {**rows, (3, 0): a_pq, (3, 2): b_pq}
    six = tile(rows, {(-3, False): c4}, [five, four])
    keep, give = tile(rows, {(-3, True): d4}, [six], spots=(0, 1, 2, 4, 3, 5, 6, 7))
    toward, back = call(
        cross_kernel, (shape(1, 1024, jnp.float32), shape(1, 128, jnp.float32)), [VMEM] * 4,
        [incoming, small, ids, target], [give], flops=2**28,
    )
    returned = pack_shift(back, -1)
    keep, give = fold(keep, over(give, "Q2"))
    keep, give = fold(keep, over(give, "P2"))
    keep, give = fold(keep, over(give, "Q"))
    giant_max = fold(keep, over(give, "P"))
    small_max = call(finish_kernel, shape(1, 1024, jnp.float32), [VMEM] * 4, [returned, send, local, toward])
    return giant_max.reshape(128), small_max.reshape(1024)


def solution(mesh):
    spread = P(AXES)
    wide = P(AXES, None)
    return jax.shard_map(
        body,
        mesh=mesh,
        in_specs=(wide, wide, spread, spread, spread),
        out_specs=(spread, spread),
        check_vma=False,
    )
```

time: 176 us -> 72.1 us (0.41)
  the two profiles are of different devices: /device:TPU:1 before, /device:TPU:6 now
where the time goes in v2:
time: 72.1 us; the launch traced here: 71.1 us
  starting transfers between devices  30.7 us (43%)
  waiting for transfers between devices  21.4 us (30%)
  Pallas kernels  15.7 us (22%)
  local copies, waits for them, and re-layouts  2.55 us (4%)
  between operations  0.8 us (1%)
    ppermute x17, starting transfers between devices, over(): lax.ppermute(block, AXES, route(lambda x, y, z, c: (*partner(link, x, y,...  28 us
    ppermute x17, waiting for transfers between devices, over(): lax.ppermute(block, AXES, route(lambda x, y, z, c: (*partner(link, x, y,...  21.2 us
    pallas_call x21, Pallas kernels, call(): pl.pallas_call(run, out_shape=out_shape, in_specs=list(specs) + [LATER] *...  15.7 us
    unnamed x10, local copies, waits for them, and re-layouts  2.55 us
    ppermute x2, starting transfers between devices, pack_shift(): lax.ppermute(block, 'pack', [((i - distance) % size, i) for i in range(si...  2.46 us
  transfers between devices with their start and end apart: 23, of which 12 were waited for; matrix products, arithmetic and copies ran while one was open for 0% of the time, Pallas kernels for 21%

profile of v2, /device:TPU:6, one launch (start us, length us, event | category | flops | bytes accessed | tf_op | source)
XLA Modules:
  0.0 71.1 jit_solution(10002845099246290878)
XLA Ops:
  1.7 2.0 %collective-permute-start.1 = (bf16[128,1024]{1,0:T(8,128)(2,1)S(1)}, bf16[128,1024]{1,0:T(8,128)(2,1)S(1)}, u32[]{:S(2)}, u32[]{:S(2)}) collective-permute-start(bf16[128,1024]{1,0:T(8,128)(2,1)S(1)} %shard_map.68.refs_1_.refs_0_), channel_id=1, source_target_pairs={{0,1},{4,39},{1,0},{5,6},{2,3},{6,5},{3,2},{7,36},{32,33},{36,7},{... | collective-permute-start | bytes 786440 | tf_op jit(solution)/shard_map/ppermute | solution.py:40
  4.6 1.6 %copy-done = bf16[1024,1024]{1,0:T(8,128)(2,1)S(1)} copy-done((bf16[1024,1024]{1,0:T(8,128)(2,1)S(1)}, bf16[1024,1024]{1,0:T(8,128)(2,1)}, u32[]{:S(2)}) %copy-start) | copy-done | bytes 2097176
  6.8 1.4 %collective-permute-done.1.refs_1_ = bf16[128,1024]{1,0:T(8,128)(2,1)S(1)} collective-permute-done((bf16[128,1024]{1,0:T(8,128)(2,1)S(1)}, bf16[128,1024]{1,0:T(8,128)(2,1)S(1)}, u32[]{:S(2)}, u32[]{:S(2)}) %collective-permute-start.1) | collective-permute-done | bytes 262176 | tf_op jit(solution)/shard_map/ppermute | solution.py:40
  8.2 5.9 %collective-permute-start.10 = (bf16[256,1024]{1,0:T(8,128)(2,1)S(1)}, bf16[256,1024]{1,0:T(8,128)(2,1)S(1)}, u32[]{:S(2)}, u32[]{:S(2)}) collective-permute-start(bf16[256,1024]{1,0:T(8,128)(2,1)S(1)} %shard_map.70.refs_2_), channel_id=1, source_target_pairs={{0,35},{4,5},{1,2},{5,4},{2,1},{6,7},{3,32},{7,6},{32,3},{36,37},{... | collective-permute-start | bytes 1572872 | tf_op jit(solution)/shard_map/ppermute | solution.py:40
  14.2 3.1 %collective-permute-start.5 = (bf16[256,1024]{1,0:T(8,128)(2,1)S(1)}, bf16[256,1024]{1,0:T(8,128)(2,1)S(1)}, u32[]{:S(2)}, u32[]{:S(2)}) collective-permute-start(bf16[256,1024]{1,0:T(8,128)(2,1)S(1)} %shard_map.71.refs_2_.refs_0_), channel_id=1, source_target_pairs={{0,192},{4,28},{1,193},{5,29},{2,194},{6,30},{3,195},{7,31},{32,22... | collective-permute-start | bytes 1572872 | tf_op jit(solution)/shard_map/ppermute | solution.py:40
  17.8 2.8 %collective-permute-start.3 = (bf16[128,1024]{1,0:T(8,128)(2,1)S(1)}, bf16[128,1024]{1,0:T(8,128)(2,1)S(1)}, u32[]{:S(2)}, u32[]{:S(2)}) collective-permute-start(bf16[128,1024]{1,0:T(8,128)(2,1)S(1)} %collective-permute-done.refs_1_), channel_id=1, source_target_pairs={{0,24},{4,196},{1,25},{5,197},{2,26},{6,198},{3,27},{7,199},{32,56... | collective-permute-start | bytes 786440 | tf_op jit(solution)/shard_map/ppermute | solution.py:40
  21.3 1.6 %shard_map.72.refs_2_ = f32[1,1024]{1,0:T(1,128)S(1)} custom-call(bf16[1024,1024]{1,0:T(8,128)(2,1)S(1)} %shard_map.69.refs_2_.refs_0_.refs_1_, s32[1,1024]{1,0:T(1,128)S(1)} %bitcast.5, bf16[256,1024]{1,0:T(8,128)(2,1)S(1)} %shard_map.71.refs_2_.refs_0_), custom_call_target="tpu_custom_call" | custom-call | flops 1342177280 | tf_op jit(solution)/shard_map/pallas_call | solution.py:54
  22.9 1.9 %collective-permute-done.2.refs_0_ = bf16[128,1024]{1,0:T(8,128)(2,1)S(1)} collective-permute-done((bf16[128,1024]{1,0:T(8,128)(2,1)S(1)}, bf16[128,1024]{1,0:T(8,128)(2,1)S(1)}, u32[]{:S(2)}, u32[]{:S(2)}) %collective-permute-start.2) | collective-permute-done | bytes 262176 | tf_op jit(solution)/shard_map/ppermute | solution.py:40
  24.9 2.8 %collective-permute-done.3.refs_1_ = bf16[128,1024]{1,0:T(8,128)(2,1)S(1)} collective-permute-done((bf16[128,1024]{1,0:T(8,128)(2,1)S(1)}, bf16[128,1024]{1,0:T(8,128)(2,1)S(1)}, u32[]{:S(2)}, u32[]{:S(2)}) %collective-permute-start.3) | collective-permute-done | bytes 262176 | tf_op jit(solution)/shard_map/ppermute | solution.py:40
  27.7 3.0 %collective-permute-start.7 = (bf16[256,1024]{1,0:T(8,128)(2,1)S(1)}, bf16[256,1024]{1,0:T(8,128)(2,1)S(1)}, u32[]{:S(2)}, u32[]{:S(2)}) collective-permute-start(bf16[256,1024]{1,0:T(8,128)(2,1)S(1)} %shard_map.73.refs_2_.refs_1_), channel_id=1, source_target_pairs={{0,192},{4,28},{1,193},{5,29},{2,194},{6,30},{3,195},{7,31},{32,22... | collective-permute-start | bytes 1572872 | tf_op jit(solution)/shard_map/ppermute | solution.py:40
  31.0 2.7 %collective-permute-start.12 = (bf16[256,1024]{1,0:T(8,128)(2,1)S(1)}, bf16[256,1024]{1,0:T(8,128)(2,1)S(1)}, u32[]{:S(2)}, u32[]{:S(2)}) collective-permute-start(bf16[256,1024]{1,0:T(8,128)(2,1)S(1)} %collective-permute-done.11.refs_6_), channel_id=1, source_target_pairs={{0,35},{4,5},{1,2},{5,4},{2,1},{6,7},{3,32},{7,6},{32,3},{36,37},{... | collective-permute-start | bytes 1572872 | tf_op jit(solution)/shard_map/ppermute | solution.py:40
  33.7 3.0 %collective-permute-start.8 = (bf16[256,1024]{1,0:T(8,128)(2,1)S(1)}, bf16[256,1024]{1,0:T(8,128)(2,1)S(1)}, u32[]{:S(2)}, u32[]{:S(2)}) collective-permute-start(bf16[256,1024]{1,0:T(8,128)(2,1)S(1)} %collective-permute-done.4.refs_0_.refs_2_), channel_id=1, source_target_pairs={{0,192},{4,28},{1,193},{5,29},{2,194},{6,30},{3,195},{7,31},{32,22... | collective-permute-start | bytes 1572872 | tf_op jit(solution)/shard_map/ppermute | solution.py:40
  36.8 1.5 %collective-permute-done.7.refs_1_.refs_5_ = bf16[256,1024]{1,0:T(8,128)(2,1)S(1)} collective-permute-done((bf16[256,1024]{1,0:T(8,128)(2,1)S(1)}, bf16[256,1024]{1,0:T(8,128)(2,1)S(1)}, u32[]{:S(2)}, u32[]{:S(2)}) %collective-permute-start.7) | collective-permute-done | bytes 524320 | tf_op jit(solution)/shard_map/ppermute | solution.py:40
  39.8 1.3 %shard_map.76.refs_6_.refs_9_ = f32[4,128]{1,0:T(4,128)S(1)} custom-call(bf16[256,1024]{1,0:T(8,128)(2,1)S(1)} %collective-permute-done.4.refs_0_.refs_2_, bf16[256,1024]{1,0:T(8,128)(2,1)S(1)} %collective-permute-done.5.refs_1_.refs_3_, bf16[256,1024]{1,0:T(8,128)(2,1)S(1)} %shard_map.70.refs_2_, bf16[256,1024]{1,0:T(8,128)(2,1)S(1)} %collective-permute-done.16.refs_3_, ...), custom_call_target="tpu_custom_call" | custom-call | flops 1073741824 | bytes 3145728 | tf_op jit(solution)/shard_map/pallas_call | solution.py:54
  41.8 1.3 %shard_map.77.refs_5_.refs_10_ = f32[4,128]{1,0:T(4,128)S(1)} custom-call(bf16[256,1024]{1,0:T(8,128)(2,1)S(1)} %collective-permute-done.6.refs_0_.refs_4_, bf16[256,1024]{1,0:T(8,128)(2,1)S(1)} %collective-permute-done.7.refs_1_.refs_5_, bf16[256,1024]{1,0:T(8,128)(2,1)S(1)} %shard_map.70.refs_2_, bf16[256,1024]{1,0:T(8,128)(2,1)S(1)} %collective-permute-done.16.refs_3_, ...), custom_call_target="tpu_custom_call" | custom-call | flops 1073741824 | bytes 3145728 | tf_op jit(solution)/shard_map/pallas_call | solution.py:54
  44.1 3.3 %collective-permute-done.9.refs_1_.refs_7_ = bf16[256,1024]{1,0:T(8,128)(2,1)S(1)} collective-permute-done((bf16[256,1024]{1,0:T(8,128)(2,1)S(1)}, bf16[256,1024]{1,0:T(8,128)(2,1)S(1)}, u32[]{:S(2)}, u32[]{:S(2)}) %collective-permute-start.9) | collective-permute-done | bytes 524320 | tf_op jit(solution)/shard_map/ppermute | solution.py:40
  47.4 1.9 %shard_map.79.refs_11_.refs_10_ = f32[4,128]{1,0:T(4,128)S(1)} custom-call(bf16[256,1024]{1,0:T(8,128)(2,1)S(1)} %collective-permute-done.8.refs_0_.refs_6_, bf16[256,1024]{1,0:T(8,128)(2,1)S(1)} %collective-permute-done.9.refs_1_.refs_7_, bf16[256,1024]{1,0:T(8,128)(2,1)S(1)} %shard_map.70.refs_2_, bf16[256,1024]{1,0:T(8,128)(2,1)S(1)} %collective-permute-done.16.refs_3_, ...), custom_call_target="tpu_custom_call" | custom-call | flops 1610612736 | bytes 4194304 | tf_op jit(solution)/shard_map/pallas_call | solution.py:54
  49.3 1.9 %shard_map.80.refs_9_ = f32[12,128]{1,0:T(8,128)S(1)} custom-call(bf16[256,1024]{1,0:T(8,128)(2,1)S(1)} %shard_map.71.refs_2_.refs_0_, bf16[256,1024]{1,0:T(8,128)(2,1)S(1)} %shard_map.73.refs_2_.refs_1_, bf16[256,1024]{1,0:T(8,128)(2,1)S(1)} %collective-permute-done.4.refs_0_.refs_2_, bf16[256,1024]{1,0:T(8,128)(2,1)S(1)} %collective-permute-done.5.refs_1_.refs_3_, ...), custom_call_target="tpu_custom_call" | custom-call | flops 1610612736 | bytes 4194304 | tf_op jit(solution)/shard_map/pallas_call | solution.py:54
  53.8 3.0 %collective-permute-start.17 = (f32[8,128]{1,0:T(8,128)S(1)}, f32[8,128]{1,0:T(8,128)S(1)}, u32[]{:S(2)}, u32[]{:S(2)}) collective-permute-start(f32[8,128]{1,0:T(8,128)S(1)} %get-tuple-element.13.refs_4_), channel_id=1, source_target_pairs={{0,192},{4,28},{1,193},{5,29},{2,194},{6,30},{3,195},{7,31},{32,22... | collective-permute-start | bytes 12296 | tf_op jit(solution)/shard_map/ppermute | solution.py:40
  56.8 1.9 %collective-permute-done.17.refs_1_ = f32[8,128]{1,0:T(8,128)S(1)} collective-permute-done((f32[8,128]{1,0:T(8,128)S(1)}, f32[8,128]{1,0:T(8,128)S(1)}, u32[]{:S(2)}, u32[]{:S(2)}) %collective-permute-start.17) | collective-permute-done | bytes 4128 | tf_op jit(solution)/shard_map/ppermute | solution.py:40
  58.7 3.6 %collective-permute-done.18.refs_1_ = f32[4,128]{1,0:T(4,128)S(1)} collective-permute-done((f32[4,128]{1,0:T(4,128)S(1)}, f32[4,128]{1,0:T(4,128)S(1)}, u32[]{:S(2)}, u32[]{:S(2)}) %collective-permute-start.18) | collective-permute-done | bytes 2080 | tf_op jit(solution)/shard_map/ppermute | solution.py:40
  63.7 2.0 %collective-permute-start.22 = (f32[1,128]{1,0:T(1,128)S(1)}, f32[1,128]{1,0:T(1,128)S(1)}, u32[]{:S(2)}, u32[]{:S(2)}) collective-permute-start(f32[1,128]{1,0:T(1,128)S(1)} %get-tuple-element.20), channel_id=1, source_target_pairs={{1,0},{2,1},{3,2},{0,3},{5,4},{6,5},{7,6},{4,7},{9,8},{10,9},{11,1... | collective-permute-start | bytes 1544 | tf_op jit(solution)/shard_map/ppermute | solution.py:244
  65.7 1.4 %collective-permute-done.19.refs_1_ = f32[2,128]{1,0:T(2,128)S(1)} collective-permute-done((f32[2,128]{1,0:T(2,128)S(1)}, f32[2,128]{1,0:T(2,128)S(1)}, u32[]{:S(2)}, u32[]{:S(2)}) %collective-permute-start.19) | collective-permute-done | bytes 1056 | tf_op jit(solution)/shard_map/ppermute | solution.py:40
  68.0 2.6 %collective-permute-done.20.refs_1_ = f32[1,128]{1,0:T(1,128)S(1)} collective-permute-done((f32[1,128]{1,0:T(1,128)S(1)}, f32[1,128]{1,0:T(1,128)S(1)}, u32[]{:S(2)}, u32[]{:S(2)}) %collective-permute-start.20) | collective-permute-done | bytes 544 | tf_op jit(solution)/shard_map/ppermute | solution.py:40
  (53 shorter events, 12.9 us)
Async XLA Ops:
  1.7 6.5 %collective-permute-start.1 = (bf16[128,1024]{1,0:T(8,128)(2,1)S(1)}, bf16[128,1024]{1,0:T(8,128)(2,1)S(1)}, u32[]{:S(2)}, u32[]{:S(2)}) collective-permute-start(bf16[128,1024]{1,0:T(8,128)(2,1)S(1)} %shard_map.68.refs_1_.refs_0_), channel_id=1, source_target_pairs={{0,1},{4,39},{1,0},{5,6},{2,3},{6,5},{3,2},{7,36},{32,33},{36,7},{... | collective-permute-start | bytes 786440 | tf_op jit(solution)/shard_map/ppermute | solution.py:40
  3.7 10.4 %collective-permute-start = (bf16[128,1024]{1,0:T(8,128)(2,1)S(1)}, bf16[128,1024]{1,0:T(8,128)(2,1)S(1)}, u32[]{:S(2)}, u32[]{:S(2)}) collective-permute-start(bf16[128,1024]{1,0:T(8,128)(2,1)S(1)} %shard_map.68.refs_1_.refs_0_), channel_id=1, source_target_pairs={{0,8},{4,68},{1,9},{5,69},{2,10},{6,70},{3,11},{7,71},{32,40},{36,... | collective-permute-start | bytes 786440 | tf_op jit(solution)/shard_map/ppermute | solution.py:40
  8.2 13.1 %collective-permute-start.10 = (bf16[256,1024]{1,0:T(8,128)(2,1)S(1)}, bf16[256,1024]{1,0:T(8,128)(2,1)S(1)}, u32[]{:S(2)}, u32[]{:S(2)}) collective-permute-start(bf16[256,1024]{1,0:T(8,128)(2,1)S(1)} %shard_map.70.refs_2_), channel_id=1, source_target_pairs={{0,35},{4,5},{1,2},{5,4},{2,1},{6,7},{3,32},{7,6},{32,3},{36,37},{... | collective-permute-start | bytes 1572872 | tf_op jit(solution)/shard_map/ppermute | solution.py:40
  14.2 16.5 %collective-permute-start.5 = (bf16[256,1024]{1,0:T(8,128)(2,1)S(1)}, bf16[256,1024]{1,0:T(8,128)(2,1)S(1)}, u32[]{:S(2)}, u32[]{:S(2)}) collective-permute-start(bf16[256,1024]{1,0:T(8,128)(2,1)S(1)} %shard_map.71.refs_2_.refs_0_), channel_id=1, source_target_pairs={{0,192},{4,28},{1,193},{5,29},{2,194},{6,30},{3,195},{7,31},{32,22... | collective-permute-start | bytes 1572872 | tf_op jit(solution)/shard_map/ppermute | solution.py:40
  17.3 7.6 %collective-permute-start.2 = (bf16[128,1024]{1,0:T(8,128)(2,1)S(1)}, bf16[128,1024]{1,0:T(8,128)(2,1)S(1)}, u32[]{:S(2)}, u32[]{:S(2)}) collective-permute-start(bf16[128,1024]{1,0:T(8,128)(2,1)S(1)} %shard_map.68.refs_1_.refs_0_), channel_id=1, source_target_pairs={{0,24},{4,196},{1,25},{5,197},{2,26},{6,198},{3,27},{7,199},{32,56... | collective-permute-start | bytes 786440 | tf_op jit(solution)/shard_map/ppermute | solution.py:40
  17.8 9.9 %collective-permute-start.3 = (bf16[128,1024]{1,0:T(8,128)(2,1)S(1)}, bf16[128,1024]{1,0:T(8,128)(2,1)S(1)}, u32[]{:S(2)}, u32[]{:S(2)}) collective-permute-start(bf16[128,1024]{1,0:T(8,128)(2,1)S(1)} %collective-permute-done.refs_1_), channel_id=1, source_target_pairs={{0,24},{4,196},{1,25},{5,197},{2,26},{6,198},{3,27},{7,199},{32,56... | collective-permute-start | bytes 786440 | tf_op jit(solution)/shard_map/ppermute | solution.py:40
  20.5 10.2 %collective-permute-start.4 = (bf16[256,1024]{1,0:T(8,128)(2,1)S(1)}, bf16[256,1024]{1,0:T(8,128)(2,1)S(1)}, u32[]{:S(2)}, u32[]{:S(2)}) collective-permute-start(bf16[256,1024]{1,0:T(8,128)(2,1)S(1)} %shard_map.71.refs_2_.refs_0_), channel_id=1, source_target_pairs={{0,64},{4,12},{1,65},{5,13},{2,66},{6,14},{3,67},{7,15},{32,96},{3... | collective-permute-start | bytes 1572872 | tf_op jit(solution)/shard_map/ppermute | solution.py:40
  21.3 9.7 %collective-permute-start.11 = (bf16[256,1024]{1,0:T(8,128)(2,1)S(1)}, bf16[256,1024]{1,0:T(8,128)(2,1)S(1)}, u32[]{:S(2)}, u32[]{:S(2)}) collective-permute-start(bf16[256,1024]{1,0:T(8,128)(2,1)S(1)} %collective-permute-done.10.refs_4_.refs_2_), channel_id=1, source_target_pairs={{0,1},{4,39},{1,0},{5,6},{2,3},{6,5},{3,2},{7,36},{32,33},{36,7},{... | collective-permute-start | bytes 1572872 | tf_op jit(solution)/shard_map/ppermute | solution.py:40
  21.3 17.2 %copy-start.3 = (s32[128]{0:T(128)S(1)}, s32[128]{0:T(128)}, u32[]{:S(2)}) copy-start(s32[128]{0:T(128)} %param.8) | copy-start | bytes 1540
  24.9 8.8 %collective-permute-start.16 = (bf16[256,1024]{1,0:T(8,128)(2,1)S(1)}, bf16[256,1024]{1,0:T(8,128)(2,1)S(1)}, u32[]{:S(2)}, u32[]{:S(2)}) collective-permute-start(bf16[256,1024]{1,0:T(8,128)(2,1)S(1)} %shard_map.70.refs_2_), channel_id=1, source_target_pairs={{0,4},{4,0},{1,5},{5,1},{2,6},{6,2},{3,7},{7,3},{32,36},{36,32},{3... | collective-permute-start | bytes 1572872 | tf_op jit(solution)/shard_map/ppermute | solution.py:44
  27.7 10.5 %collective-permute-start.7 = (bf16[256,1024]{1,0:T(8,128)(2,1)S(1)}, bf16[256,1024]{1,0:T(8,128)(2,1)S(1)}, u32[]{:S(2)}, u32[]{:S(2)}) collective-permute-start(bf16[256,1024]{1,0:T(8,128)(2,1)S(1)} %shard_map.73.refs_2_.refs_1_), channel_id=1, source_target_pairs={{0,192},{4,28},{1,193},{5,29},{2,194},{6,30},{3,195},{7,31},{32,22... | collective-permute-start | bytes 1572872 | tf_op jit(solution)/shard_map/ppermute | solution.py:40
  30.8 7.7 %collective-permute-start.15 = (bf16[256,1024]{1,0:T(8,128)(2,1)S(1)}, bf16[256,1024]{1,0:T(8,128)(2,1)S(1)}, u32[]{:S(2)}, u32[]{:S(2)}) collective-permute-start(bf16[256,1024]{1,0:T(8,128)(2,1)S(1)} %collective-permute-done.10.refs_4_.refs_2_), channel_id=1, source_target_pairs={{0,4},{4,0},{1,5},{5,1},{2,6},{6,2},{3,7},{7,3},{32,36},{36,32},{3... | collective-permute-start | bytes 1572872 | tf_op jit(solution)/shard_map/ppermute | solution.py:44
  30.8 10.4 %collective-permute-start.6 = (bf16[256,1024]{1,0:T(8,128)(2,1)S(1)}, bf16[256,1024]{1,0:T(8,128)(2,1)S(1)}, u32[]{:S(2)}, u32[]{:S(2)}) collective-permute-start(bf16[256,1024]{1,0:T(8,128)(2,1)S(1)} %shard_map.73.refs_2_.refs_1_), channel_id=1, source_target_pairs={{0,64},{4,12},{1,65},{5,13},{2,66},{6,14},{3,67},{7,15},{32,96},{3... | collective-permute-start | bytes 1572872 | tf_op jit(solution)/shard_map/ppermute | solution.py:40
  31.0 10.6 %collective-permute-start.12 = (bf16[256,1024]{1,0:T(8,128)(2,1)S(1)}, bf16[256,1024]{1,0:T(8,128)(2,1)S(1)}, u32[]{:S(2)}, u32[]{:S(2)}) collective-permute-start(bf16[256,1024]{1,0:T(8,128)(2,1)S(1)} %collective-permute-done.11.refs_6_), channel_id=1, source_target_pairs={{0,35},{4,5},{1,2},{5,4},{2,1},{6,7},{3,32},{7,6},{32,3},{36,37},{... | collective-permute-start | bytes 1572872 | tf_op jit(solution)/shard_map/ppermute | solution.py:40
  33.7 10.4 %collective-permute-start.8 = (bf16[256,1024]{1,0:T(8,128)(2,1)S(1)}, bf16[256,1024]{1,0:T(8,128)(2,1)S(1)}, u32[]{:S(2)}, u32[]{:S(2)}) collective-permute-start(bf16[256,1024]{1,0:T(8,128)(2,1)S(1)} %collective-permute-done.4.refs_0_.refs_2_), channel_id=1, source_target_pairs={{0,192},{4,28},{1,193},{5,29},{2,194},{6,30},{3,195},{7,31},{32,22... | collective-permute-start | bytes 1572872 | tf_op jit(solution)/shard_map/ppermute | solution.py:40
  38.2 9.2 %collective-permute-start.9 = (bf16[256,1024]{1,0:T(8,128)(2,1)S(1)}, bf16[256,1024]{1,0:T(8,128)(2,1)S(1)}, u32[]{:S(2)}, u32[]{:S(2)}) collective-permute-start(bf16[256,1024]{1,0:T(8,128)(2,1)S(1)} %collective-permute-done.7.refs_1_.refs_5_), channel_id=1, source_target_pairs={{0,64},{4,12},{1,65},{5,13},{2,66},{6,14},{3,67},{7,15},{32,96},{3... | collective-permute-start | bytes 1572872 | tf_op jit(solution)/shard_map/ppermute | solution.py:40
  38.5 8.9 %collective-permute-start.14 = (bf16[256,1024]{1,0:T(8,128)(2,1)S(1)}, bf16[256,1024]{1,0:T(8,128)(2,1)S(1)}, u32[]{:S(2)}, u32[]{:S(2)}) collective-permute-start(bf16[256,1024]{1,0:T(8,128)(2,1)S(1)} %collective-permute-done.11.refs_6_), channel_id=1, source_target_pairs={{0,4},{4,0},{1,5},{5,1},{2,6},{6,2},{3,7},{7,3},{32,36},{36,32},{3... | collective-permute-start | bytes 1572872 | tf_op jit(solution)/shard_map/ppermute | solution.py:44
  41.1 21.7 %collective-permute-start.21 = (bf16[128,1024]{1,0:T(8,128)(2,1)S(1)}, bf16[128,1024]{1,0:T(8,128)(2,1)S(1)}, u32[]{:S(2)}, u32[]{:S(2)}) collective-permute-start(bf16[128,1024]{1,0:T(8,128)(2,1)S(1)} %shard_map.74.refs_4_), channel_id=1, source_target_pairs={{3,0},{0,1},{1,2},{2,3},{7,4},{4,5},{5,6},{6,7},{11,8},{8,9},{9,10... | collective-permute-start | bytes 786440 | tf_op jit(solution)/shard_map/ppermute | solution.py:244
  41.6 10.9 %collective-permute-start.13 = (bf16[256,1024]{1,0:T(8,128)(2,1)S(1)}, bf16[256,1024]{1,0:T(8,128)(2,1)S(1)}, u32[]{:S(2)}, u32[]{:S(2)}) collective-permute-start(bf16[256,1024]{1,0:T(8,128)(2,1)S(1)} %collective-permute-done.12.refs_8_), channel_id=1, source_target_pairs={{0,4},{4,0},{1,5},{5,1},{2,6},{6,2},{3,7},{7,3},{32,36},{36,32},{3... | collective-permute-start | bytes 1572872 | tf_op jit(solution)/shard_map/ppermute | solution.py:44
  53.8 4.9 %collective-permute-start.17 = (f32[8,128]{1,0:T(8,128)S(1)}, f32[8,128]{1,0:T(8,128)S(1)}, u32[]{:S(2)}, u32[]{:S(2)}) collective-permute-start(f32[8,128]{1,0:T(8,128)S(1)} %get-tuple-element.13.refs_4_), channel_id=1, source_target_pairs={{0,192},{4,28},{1,193},{5,29},{2,194},{6,30},{3,195},{7,31},{32,22... | collective-permute-start | bytes 12296 | tf_op jit(solution)/shard_map/ppermute | solution.py:40
  58.7 3.6 %collective-permute-start.18 = (f32[4,128]{1,0:T(4,128)S(1)}, f32[4,128]{1,0:T(4,128)S(1)}, u32[]{:S(2)}, u32[]{:S(2)}) collective-permute-start(f32[4,128]{1,0:T(4,128)S(1)} %get-tuple-element.15), channel_id=1, source_target_pairs={{0,64},{4,12},{1,65},{5,13},{2,66},{6,14},{3,67},{7,15},{32,96},{3... | collective-permute-start | bytes 6152 | tf_op jit(solution)/shard_map/ppermute | solution.py:40
  62.3 4.8 %collective-permute-start.19 = (f32[2,128]{1,0:T(2,128)S(1)}, f32[2,128]{1,0:T(2,128)S(1)}, u32[]{:S(2)}, u32[]{:S(2)}) collective-permute-start(f32[2,128]{1,0:T(2,128)S(1)} %get-tuple-element.17), channel_id=1, source_target_pairs={{0,24},{4,196},{1,25},{5,197},{2,26},{6,198},{3,27},{7,199},{32,56... | collective-permute-start | bytes 3080 | tf_op jit(solution)/shard_map/ppermute | solution.py:40
  63.7 3.6 %collective-permute-start.22 = (f32[1,128]{1,0:T(1,128)S(1)}, f32[1,128]{1,0:T(1,128)S(1)}, u32[]{:S(2)}, u32[]{:S(2)}) collective-permute-start(f32[1,128]{1,0:T(1,128)S(1)} %get-tuple-element.20), channel_id=1, source_target_pairs={{1,0},{2,1},{3,2},{0,3},{5,4},{6,5},{7,6},{4,7},{9,8},{10,9},{11,1... | collective-permute-start | bytes 1544 | tf_op jit(solution)/shard_map/ppermute | solution.py:244
  67.1 3.5 %collective-permute-start.20 = (f32[1,128]{1,0:T(1,128)S(1)}, f32[1,128]{1,0:T(1,128)S(1)}, u32[]{:S(2)}, u32[]{:S(2)}) collective-permute-start(f32[1,128]{1,0:T(1,128)S(1)} %get-tuple-element.19), channel_id=1, source_target_pairs={{0,8},{4,68},{1,9},{5,69},{2,10},{6,70},{3,11},{7,71},{32,40},{36,... | collective-permute-start | bytes 1544 | tf_op jit(solution)/shard_map/ppermute | solution.py:40
  (4 other events, 27.4 us)

commit v3 on v2

--- a/solution.py
+++ b/solution.py
@@ -252,7 +252,7 @@
     small = call(unit_kernel, shape(1024, 1024, jnp.bfloat16), [VMEM], [small_emb], [own], size=4 * MIB)
     c1 = join(own, e, [small])
     c2, d1 = over(c1, "O"), core_swap(c1)
-    a = join(own, p, [c1])
+    a = join(own, p, [c1, q])
     pq = over(p, "Q")
     a_p, a_q = over(a, "P2"), over(a, "Q2")
     local = call(local_kernel, shape(1, 1024, jnp.float32), [VMEM] * 2, [small, ids], [a], flops=20 * 2**26)

time: 72.1 us -> 71.1 us (0.986); the launches traced: 71.1 us -> 71 us
  starting transfers between devices: 30.7 us -> 24.7 us
  waiting for transfers between devices: 21.4 us -> 27.3 us
    ppermute x17, starting transfers between devices: 28 us -> 21 us  [over(): lax.ppermute(block, AXES, route(lambda x, y, z, c: (*partner(link, x, y,...]
    ppermute x17, waiting for transfers between devices: 21.2 us -> 27 us  [over(): lax.ppermute(block, AXES, route(lambda x, y, z, c: (*partner(link, x, y,...]
    ppermute x4, starting transfers between devices: 0.22 us -> 1.56 us  [core_swap(): return lax.ppermute(block, AXES, route(lambda x, y, z, c: (x, y, z, 1 - c)))]
  transfers between devices with their start and end apart: 23 -> 23, of which waited for: 12 -> 13; matrix products, arithmetic and copies ran while one was open for 0% -> 0% of each run, Pallas kernels for 21% -> 21%
where the time goes in v3:
time: 71.1 us; the launch traced here: 71 us
  waiting for transfers between devices  27.3 us (38%)
  starting transfers between devices  24.7 us (35%)
  Pallas kernels  15.7 us (22%)
  local copies, waits for them, and re-layouts  2.55 us (4%)
  between operations  0.81 us (1%)
    ppermute x17, waiting for transfers between devices, over(): lax.ppermute(block, AXES, route(lambda x, y, z, c: (*partner(link, x, y,...  27 us
    ppermute x17, starting transfers between devices, over(): lax.ppermute(block, AXES, route(lambda x, y, z, c: (*partner(link, x, y,...  21 us
    pallas_call x21, Pallas kernels, call(): pl.pallas_call(run, out_shape=out_shape, in_specs=list(specs) + [LATER] *...  15.7 us
    unnamed x10, local copies, waits for them, and re-layouts  2.55 us
    ppermute x2, starting transfers between devices, pack_shift(): lax.ppermute(block, 'pack', [((i - distance) % size, i) for i in range(si...  2.06 us
    ppermute x4, starting transfers between devices, core_swap(): return lax.ppermute(block, AXES, route(lambda x, y, z, c: (x, y, z, 1 - c)))  1.56 us
  transfers between devices with their start and end apart: 23, of which 13 were waited for; matrix products, arithmetic and copies ran while one was open for 0% of the time, Pallas kernels for 21%

profile of v3, /device:TPU:6, one launch (start us, length us, event | category | flops | bytes accessed | tf_op | source)
XLA Modules:
  0.0 71.0 jit_solution(15291331859109764605)
XLA Ops:
  1.7 2.0 %collective-permute-start.1 = (bf16[128,1024]{1,0:T(8,128)(2,1)S(1)}, bf16[128,1024]{1,0:T(8,128)(2,1)S(1)}, u32[]{:S(2)}, u32[]{:S(2)}) collective-permute-start(bf16[128,1024]{1,0:T(8,128)(2,1)S(1)} %shard_map.68.refs_1_.refs_0_), channel_id=1, source_target_pairs={{0,1},{4,39},{1,0},{5,6},{2,3},{6,5},{3,2},{7,36},{32,33},{36,7},{... | collective-permute-start | bytes 786440 | tf_op jit(solution)/shard_map/ppermute | solution.py:40
  5.1 1.6 %copy-done = bf16[1024,1024]{1,0:T(8,128)(2,1)S(1)} copy-done((bf16[1024,1024]{1,0:T(8,128)(2,1)S(1)}, bf16[1024,1024]{1,0:T(8,128)(2,1)}, u32[]{:S(2)}) %copy-start) | copy-done | bytes 2097176
  8.2 5.9 %collective-permute-start.10 = (bf16[256,1024]{1,0:T(8,128)(2,1)S(1)}, bf16[256,1024]{1,0:T(8,128)(2,1)S(1)}, u32[]{:S(2)}, u32[]{:S(2)}) collective-permute-start(bf16[256,1024]{1,0:T(8,128)(2,1)S(1)} %shard_map.70.refs_2_), channel_id=1, source_target_pairs={{0,35},{4,5},{1,2},{5,4},{2,1},{6,7},{3,32},{7,6},{32,3},{36,37},{... | collective-permute-start | bytes 1572872 | tf_op jit(solution)/shard_map/ppermute | solution.py:40
  14.2 3.1 %collective-permute-start.5 = (bf16[256,1024]{1,0:T(8,128)(2,1)S(1)}, bf16[256,1024]{1,0:T(8,128)(2,1)S(1)}, u32[]{:S(2)}, u32[]{:S(2)}) collective-permute-start(bf16[256,1024]{1,0:T(8,128)(2,1)S(1)} %shard_map.71.refs_2_.refs_0_), channel_id=1, source_target_pairs={{0,192},{4,28},{1,193},{5,29},{2,194},{6,30},{3,195},{7,31},{32,22... | collective-permute-start | bytes 1572872 | tf_op jit(solution)/shard_map/ppermute | solution.py:40
  17.9 3.4 %collective-permute-done.10.refs_4_.refs_2_ = bf16[256,1024]{1,0:T(8,128)(2,1)S(1)} collective-permute-done((bf16[256,1024]{1,0:T(8,128)(2,1)S(1)}, bf16[256,1024]{1,0:T(8,128)(2,1)S(1)}, u32[]{:S(2)}, u32[]{:S(2)}) %collective-permute-start.10) | collective-permute-done | bytes 524320 | tf_op jit(solution)/shard_map/ppermute | solution.py:40
  21.3 1.1 %collective-permute-start.16 = (bf16[256,1024]{1,0:T(8,128)(2,1)S(1)}, bf16[256,1024]{1,0:T(8,128)(2,1)S(1)}, u32[]{:S(2)}, u32[]{:S(2)}) collective-permute-start(bf16[256,1024]{1,0:T(8,128)(2,1)S(1)} %shard_map.70.refs_2_), channel_id=1, source_target_pairs={{0,4},{4,0},{1,5},{5,1},{2,6},{6,2},{3,7},{7,3},{32,36},{36,32},{3... | collective-permute-start | bytes 1572872 | tf_op jit(solution)/shard_map/ppermute | solution.py:44
  22.4 1.6 %shard_map.72.refs_2_ = f32[1,1024]{1,0:T(1,128)S(1)} custom-call(bf16[1024,1024]{1,0:T(8,128)(2,1)S(1)} %shard_map.69.refs_2_.refs_0_.refs_1_, s32[1,1024]{1,0:T(1,128)S(1)} %bitcast.5, bf16[256,1024]{1,0:T(8,128)(2,1)S(1)} %shard_map.71.refs_2_.refs_0_), custom_call_target="tpu_custom_call" | custom-call | flops 1342177280 | tf_op jit(solution)/shard_map/pallas_call | solution.py:54
  24.0 3.5 %collective-permute-done.3.refs_1_ = bf16[128,1024]{1,0:T(8,128)(2,1)S(1)} collective-permute-done((bf16[128,1024]{1,0:T(8,128)(2,1)S(1)}, bf16[128,1024]{1,0:T(8,128)(2,1)S(1)}, u32[]{:S(2)}, u32[]{:S(2)}) %collective-permute-start.3) | collective-permute-done | bytes 262176 | tf_op jit(solution)/shard_map/ppermute | solution.py:40
  28.3 2.2 %collective-permute-done.11.refs_6_ = bf16[256,1024]{1,0:T(8,128)(2,1)S(1)} collective-permute-done((bf16[256,1024]{1,0:T(8,128)(2,1)S(1)}, bf16[256,1024]{1,0:T(8,128)(2,1)S(1)}, u32[]{:S(2)}, u32[]{:S(2)}) %collective-permute-start.11) | collective-permute-done | bytes 524320 | tf_op jit(solution)/shard_map/ppermute | solution.py:40
  30.5 3.2 %collective-permute-start.12 = (bf16[256,1024]{1,0:T(8,128)(2,1)S(1)}, bf16[256,1024]{1,0:T(8,128)(2,1)S(1)}, u32[]{:S(2)}, u32[]{:S(2)}) collective-permute-start(bf16[256,1024]{1,0:T(8,128)(2,1)S(1)} %collective-permute-done.11.refs_6_), channel_id=1, source_target_pairs={{0,35},{4,5},{1,2},{5,4},{2,1},{6,7},{3,32},{7,6},{32,3},{36,37},{... | collective-permute-start | bytes 1572872 | tf_op jit(solution)/shard_map/ppermute | solution.py:40
  33.7 3.0 %collective-permute-start.8 = (bf16[256,1024]{1,0:T(8,128)(2,1)S(1)}, bf16[256,1024]{1,0:T(8,128)(2,1)S(1)}, u32[]{:S(2)}, u32[]{:S(2)}) collective-permute-start(bf16[256,1024]{1,0:T(8,128)(2,1)S(1)} %collective-permute-done.4.refs_0_.refs_2_), channel_id=1, source_target_pairs={{0,192},{4,28},{1,193},{5,29},{2,194},{6,30},{3,195},{7,31},{32,22... | collective-permute-start | bytes 1572872 | tf_op jit(solution)/shard_map/ppermute | solution.py:40
  36.8 1.3 %collective-permute-done.7.refs_1_.refs_5_ = bf16[256,1024]{1,0:T(8,128)(2,1)S(1)} collective-permute-done((bf16[256,1024]{1,0:T(8,128)(2,1)S(1)}, bf16[256,1024]{1,0:T(8,128)(2,1)S(1)}, u32[]{:S(2)}, u32[]{:S(2)}) %collective-permute-start.7) | collective-permute-done | bytes 524320 | tf_op jit(solution)/shard_map/ppermute | solution.py:40
  39.4 1.3 %shard_map.76.refs_6_.refs_9_ = f32[4,128]{1,0:T(4,128)S(1)} custom-call(bf16[256,1024]{1,0:T(8,128)(2,1)S(1)} %collective-permute-done.4.refs_0_.refs_2_, bf16[256,1024]{1,0:T(8,128)(2,1)S(1)} %collective-permute-done.5.refs_1_.refs_3_, bf16[256,1024]{1,0:T(8,128)(2,1)S(1)} %shard_map.70.refs_2_, bf16[256,1024]{1,0:T(8,128)(2,1)S(1)} %collective-permute-done.16.refs_3_, ...), custom_call_target="tpu_custom_call" | custom-call | flops 1073741824 | bytes 3145728 | tf_op jit(solution)/shard_map/pallas_call | solution.py:54
  41.4 1.3 %shard_map.77.refs_5_.refs_10_ = f32[4,128]{1,0:T(4,128)S(1)} custom-call(bf16[256,1024]{1,0:T(8,128)(2,1)S(1)} %collective-permute-done.6.refs_0_.refs_4_, bf16[256,1024]{1,0:T(8,128)(2,1)S(1)} %collective-permute-done.7.refs_1_.refs_5_, bf16[256,1024]{1,0:T(8,128)(2,1)S(1)} %shard_map.70.refs_2_, bf16[256,1024]{1,0:T(8,128)(2,1)S(1)} %collective-permute-done.16.refs_3_, ...), custom_call_target="tpu_custom_call" | custom-call | flops 1073741824 | bytes 3145728 | tf_op jit(solution)/shard_map/pallas_call | solution.py:54
  44.1 3.1 %collective-permute-done.9.refs_1_.refs_7_ = bf16[256,1024]{1,0:T(8,128)(2,1)S(1)} collective-permute-done((bf16[256,1024]{1,0:T(8,128)(2,1)S(1)}, bf16[256,1024]{1,0:T(8,128)(2,1)S(1)}, u32[]{:S(2)}, u32[]{:S(2)}) %collective-permute-start.9) | collective-permute-done | bytes 524320 | tf_op jit(solution)/shard_map/ppermute | solution.py:40
  47.2 1.9 %shard_map.79.refs_11_.refs_10_ = f32[4,128]{1,0:T(4,128)S(1)} custom-call(bf16[256,1024]{1,0:T(8,128)(2,1)S(1)} %collective-permute-done.8.refs_0_.refs_6_, bf16[256,1024]{1,0:T(8,128)(2,1)S(1)} %collective-permute-done.9.refs_1_.refs_7_, bf16[256,1024]{1,0:T(8,128)(2,1)S(1)} %shard_map.70.refs_2_, bf16[256,1024]{1,0:T(8,128)(2,1)S(1)} %collective-permute-done.16.refs_3_, ...), custom_call_target="tpu_custom_call" | custom-call | flops 1610612736 | bytes 4194304 | tf_op jit(solution)/shard_map/pallas_call | solution.py:54
  49.1 1.9 %shard_map.80.refs_9_ = f32[12,128]{1,0:T(8,128)S(1)} custom-call(bf16[256,1024]{1,0:T(8,128)(2,1)S(1)} %shard_map.71.refs_2_.refs_0_, bf16[256,1024]{1,0:T(8,128)(2,1)S(1)} %shard_map.73.refs_2_.refs_1_, bf16[256,1024]{1,0:T(8,128)(2,1)S(1)} %collective-permute-done.4.refs_0_.refs_2_, bf16[256,1024]{1,0:T(8,128)(2,1)S(1)} %collective-permute-done.5.refs_1_.refs_3_, ...), custom_call_target="tpu_custom_call" | custom-call | flops 1610612736 | bytes 4194304 | tf_op jit(solution)/shard_map/pallas_call | solution.py:54
  51.0 1.3 %shard_map.81.refs_9_ = f32[16,128]{1,0:T(8,128)S(1)} custom-call(bf16[256,1024]{1,0:T(8,128)(2,1)S(1)} %shard_map.71.refs_2_.refs_0_, bf16[256,1024]{1,0:T(8,128)(2,1)S(1)} %shard_map.73.refs_2_.refs_1_, bf16[256,1024]{1,0:T(8,128)(2,1)S(1)} %collective-permute-done.4.refs_0_.refs_2_, bf16[256,1024]{1,0:T(8,128)(2,1)S(1)} %collective-permute-done.5.refs_1_.refs_3_, ...), custom_call_target="tpu_custom_call" | custom-call | flops 1073741824 | bytes 4718592 | tf_op jit(solution)/shard_map/pallas_call | solution.py:54
  52.3 1.3 %shard_map.82 = (f32[8,128]{1,0:T(8,128)S(1)}, f32[8,128]{1,0:T(8,128)S(1)}) custom-call(bf16[256,1024]{1,0:T(8,128)(2,1)S(1)} %shard_map.71.refs_2_.refs_0_, bf16[256,1024]{1,0:T(8,128)(2,1)S(1)} %shard_map.73.refs_2_.refs_1_, bf16[256,1024]{1,0:T(8,128)(2,1)S(1)} %collective-permute-done.4.refs_0_.refs_2_, ...), custom_call_target="tpu_custom_call" | custom-call | flops 1073741824 | bytes 4718592 | tf_op jit(solution)/shard_map/pallas_call | solution.py:54
  54.2 4.4 %collective-permute-done.17.refs_1_ = f32[8,128]{1,0:T(8,128)S(1)} collective-permute-done((f32[8,128]{1,0:T(8,128)S(1)}, f32[8,128]{1,0:T(8,128)S(1)}, u32[]{:S(2)}, u32[]{:S(2)}) %collective-permute-start.17) | collective-permute-done | bytes 4128 | tf_op jit(solution)/shard_map/ppermute | solution.py:40
  58.6 3.6 %collective-permute-done.18.refs_1_ = f32[4,128]{1,0:T(4,128)S(1)} collective-permute-done((f32[4,128]{1,0:T(4,128)S(1)}, f32[4,128]{1,0:T(4,128)S(1)}, u32[]{:S(2)}, u32[]{:S(2)}) %collective-permute-start.18) | collective-permute-done | bytes 2080 | tf_op jit(solution)/shard_map/ppermute | solution.py:40
  63.5 2.0 %collective-permute-start.22 = (f32[1,128]{1,0:T(1,128)S(1)}, f32[1,128]{1,0:T(1,128)S(1)}, u32[]{:S(2)}, u32[]{:S(2)}) collective-permute-start(f32[1,128]{1,0:T(1,128)S(1)} %get-tuple-element.20), channel_id=1, source_target_pairs={{1,0},{2,1},{3,2},{0,3},{5,4},{6,5},{7,6},{4,7},{9,8},{10,9},{11,1... | collective-permute-start | bytes 1544 | tf_op jit(solution)/shard_map/ppermute | solution.py:244
  65.5 1.4 %collective-permute-done.19.refs_1_ = f32[2,128]{1,0:T(2,128)S(1)} collective-permute-done((f32[2,128]{1,0:T(2,128)S(1)}, f32[2,128]{1,0:T(2,128)S(1)}, u32[]{:S(2)}, u32[]{:S(2)}) %collective-permute-start.19) | collective-permute-done | bytes 1056 | tf_op jit(solution)/shard_map/ppermute | solution.py:40
  67.9 2.6 %collective-permute-done.20.refs_1_ = f32[1,128]{1,0:T(1,128)S(1)} collective-permute-done((f32[1,128]{1,0:T(1,128)S(1)}, f32[1,128]{1,0:T(1,128)S(1)}, u32[]{:S(2)}, u32[]{:S(2)}) %collective-permute-start.20) | collective-permute-done | bytes 544 | tf_op jit(solution)/shard_map/ppermute | solution.py:40
  (53 shorter events, 12.2 us)
Async XLA Ops:
  1.7 6.5 %collective-permute-start.1 = (bf16[128,1024]{1,0:T(8,128)(2,1)S(1)}, bf16[128,1024]{1,0:T(8,128)(2,1)S(1)}, u32[]{:S(2)}, u32[]{:S(2)}) collective-permute-start(bf16[128,1024]{1,0:T(8,128)(2,1)S(1)} %shard_map.68.refs_1_.refs_0_), channel_id=1, source_target_pairs={{0,1},{4,39},{1,0},{5,6},{2,3},{6,5},{3,2},{7,36},{32,33},{36,7},{... | collective-permute-start | bytes 786440 | tf_op jit(solution)/shard_map/ppermute | solution.py:40
  3.7 10.4 %collective-permute-start.2 = (bf16[128,1024]{1,0:T(8,128)(2,1)S(1)}, bf16[128,1024]{1,0:T(8,128)(2,1)S(1)}, u32[]{:S(2)}, u32[]{:S(2)}) collective-permute-start(bf16[128,1024]{1,0:T(8,128)(2,1)S(1)} %shard_map.68.refs_1_.refs_0_), channel_id=1, source_target_pairs={{0,24},{4,196},{1,25},{5,197},{2,26},{6,198},{3,27},{7,199},{32,56... | collective-permute-start | bytes 786440 | tf_op jit(solution)/shard_map/ppermute | solution.py:40
  4.2 10.0 %collective-permute-start = (bf16[128,1024]{1,0:T(8,128)(2,1)S(1)}, bf16[128,1024]{1,0:T(8,128)(2,1)S(1)}, u32[]{:S(2)}, u32[]{:S(2)}) collective-permute-start(bf16[128,1024]{1,0:T(8,128)(2,1)S(1)} %shard_map.68.refs_1_.refs_0_), channel_id=1, source_target_pairs={{0,8},{4,68},{1,9},{5,69},{2,10},{6,70},{3,11},{7,71},{32,40},{36,... | collective-permute-start | bytes 786440 | tf_op jit(solution)/shard_map/ppermute | solution.py:40
  8.2 13.1 %collective-permute-start.10 = (bf16[256,1024]{1,0:T(8,128)(2,1)S(1)}, bf16[256,1024]{1,0:T(8,128)(2,1)S(1)}, u32[]{:S(2)}, u32[]{:S(2)}) collective-permute-start(bf16[256,1024]{1,0:T(8,128)(2,1)S(1)} %shard_map.70.refs_2_), channel_id=1, source_target_pairs={{0,35},{4,5},{1,2},{5,4},{2,1},{6,7},{3,32},{7,6},{32,3},{36,37},{... | collective-permute-start | bytes 1572872 | tf_op jit(solution)/shard_map/ppermute | solution.py:40
  14.2 13.9 %collective-permute-start.5 = (bf16[256,1024]{1,0:T(8,128)(2,1)S(1)}, bf16[256,1024]{1,0:T(8,128)(2,1)S(1)}, u32[]{:S(2)}, u32[]{:S(2)}) collective-permute-start(bf16[256,1024]{1,0:T(8,128)(2,1)S(1)} %shard_map.71.refs_2_.refs_0_), channel_id=1, source_target_pairs={{0,192},{4,28},{1,193},{5,29},{2,194},{6,30},{3,195},{7,31},{32,22... | collective-permute-start | bytes 1572872 | tf_op jit(solution)/shard_map/ppermute | solution.py:40
  17.3 10.2 %collective-permute-start.3 = (bf16[128,1024]{1,0:T(8,128)(2,1)S(1)}, bf16[128,1024]{1,0:T(8,128)(2,1)S(1)}, u32[]{:S(2)}, u32[]{:S(2)}) collective-permute-start(bf16[128,1024]{1,0:T(8,128)(2,1)S(1)} %collective-permute-done.refs_1_), channel_id=1, source_target_pairs={{0,24},{4,196},{1,25},{5,197},{2,26},{6,198},{3,27},{7,199},{32,56... | collective-permute-start | bytes 786440 | tf_op jit(solution)/shard_map/ppermute | solution.py:40
  17.8 10.3 %collective-permute-start.4 = (bf16[256,1024]{1,0:T(8,128)(2,1)S(1)}, bf16[256,1024]{1,0:T(8,128)(2,1)S(1)}, u32[]{:S(2)}, u32[]{:S(2)}) collective-permute-start(bf16[256,1024]{1,0:T(8,128)(2,1)S(1)} %shard_map.71.refs_2_.refs_0_), channel_id=1, source_target_pairs={{0,64},{4,12},{1,65},{5,13},{2,66},{6,14},{3,67},{7,15},{32,96},{3... | collective-permute-start | bytes 1572872 | tf_op jit(solution)/shard_map/ppermute | solution.py:40
  21.3 9.2 %collective-permute-start.11 = (bf16[256,1024]{1,0:T(8,128)(2,1)S(1)}, bf16[256,1024]{1,0:T(8,128)(2,1)S(1)}, u32[]{:S(2)}, u32[]{:S(2)}) collective-permute-start(bf16[256,1024]{1,0:T(8,128)(2,1)S(1)} %collective-permute-done.10.refs_4_.refs_2_), channel_id=1, source_target_pairs={{0,1},{4,39},{1,0},{5,6},{2,3},{6,5},{3,2},{7,36},{32,33},{36,7},{... | collective-permute-start | bytes 1572872 | tf_op jit(solution)/shard_map/ppermute | solution.py:40
  21.3 12.4 %collective-permute-start.16 = (bf16[256,1024]{1,0:T(8,128)(2,1)S(1)}, bf16[256,1024]{1,0:T(8,128)(2,1)S(1)}, u32[]{:S(2)}, u32[]{:S(2)}) collective-permute-start(bf16[256,1024]{1,0:T(8,128)(2,1)S(1)} %shard_map.70.refs_2_), channel_id=1, source_target_pairs={{0,4},{4,0},{1,5},{5,1},{2,6},{6,2},{3,7},{7,3},{32,36},{36,32},{3... | collective-permute-start | bytes 1572872 | tf_op jit(solution)/shard_map/ppermute | solution.py:44
  22.4 15.7 %copy-start.3 = (s32[128]{0:T(128)S(1)}, s32[128]{0:T(128)}, u32[]{:S(2)}) copy-start(s32[128]{0:T(128)} %param.8) | copy-start | bytes 1540
  27.6 10.5 %collective-permute-start.7 = (bf16[256,1024]{1,0:T(8,128)(2,1)S(1)}, bf16[256,1024]{1,0:T(8,128)(2,1)S(1)}, u32[]{:S(2)}, u32[]{:S(2)}) collective-permute-start(bf16[256,1024]{1,0:T(8,128)(2,1)S(1)} %shard_map.73.refs_2_.refs_1_), channel_id=1, source_target_pairs={{0,192},{4,28},{1,193},{5,29},{2,194},{6,30},{3,195},{7,31},{32,22... | collective-permute-start | bytes 1572872 | tf_op jit(solution)/shard_map/ppermute | solution.py:40
  28.1 9.9 %collective-permute-start.15 = (bf16[256,1024]{1,0:T(8,128)(2,1)S(1)}, bf16[256,1024]{1,0:T(8,128)(2,1)S(1)}, u32[]{:S(2)}, u32[]{:S(2)}) collective-permute-start(bf16[256,1024]{1,0:T(8,128)(2,1)S(1)} %collective-permute-done.10.refs_4_.refs_2_), channel_id=1, source_target_pairs={{0,4},{4,0},{1,5},{5,1},{2,6},{6,2},{3,7},{7,3},{32,36},{36,32},{3... | collective-permute-start | bytes 1572872 | tf_op jit(solution)/shard_map/ppermute | solution.py:44
  28.1 12.6 %collective-permute-start.6 = (bf16[256,1024]{1,0:T(8,128)(2,1)S(1)}, bf16[256,1024]{1,0:T(8,128)(2,1)S(1)}, u32[]{:S(2)}, u32[]{:S(2)}) collective-permute-start(bf16[256,1024]{1,0:T(8,128)(2,1)S(1)} %shard_map.73.refs_2_.refs_1_), channel_id=1, source_target_pairs={{0,64},{4,12},{1,65},{5,13},{2,66},{6,14},{3,67},{7,15},{32,96},{3... | collective-permute-start | bytes 1572872 | tf_op jit(solution)/shard_map/ppermute | solution.py:40
  30.5 10.4 %collective-permute-start.12 = (bf16[256,1024]{1,0:T(8,128)(2,1)S(1)}, bf16[256,1024]{1,0:T(8,128)(2,1)S(1)}, u32[]{:S(2)}, u32[]{:S(2)}) collective-permute-start(bf16[256,1024]{1,0:T(8,128)(2,1)S(1)} %collective-permute-done.11.refs_6_), channel_id=1, source_target_pairs={{0,35},{4,5},{1,2},{5,4},{2,1},{6,7},{3,32},{7,6},{32,3},{36,37},{... | collective-permute-start | bytes 1572872 | tf_op jit(solution)/shard_map/ppermute | solution.py:40
  33.7 10.4 %collective-permute-start.8 = (bf16[256,1024]{1,0:T(8,128)(2,1)S(1)}, bf16[256,1024]{1,0:T(8,128)(2,1)S(1)}, u32[]{:S(2)}, u32[]{:S(2)}) collective-permute-start(bf16[256,1024]{1,0:T(8,128)(2,1)S(1)} %collective-permute-done.4.refs_0_.refs_2_), channel_id=1, source_target_pairs={{0,192},{4,28},{1,193},{5,29},{2,194},{6,30},{3,195},{7,31},{32,22... | collective-permute-start | bytes 1572872 | tf_op jit(solution)/shard_map/ppermute | solution.py:40
  38.1 9.2 %collective-permute-start.9 = (bf16[256,1024]{1,0:T(8,128)(2,1)S(1)}, bf16[256,1024]{1,0:T(8,128)(2,1)S(1)}, u32[]{:S(2)}, u32[]{:S(2)}) collective-permute-start(bf16[256,1024]{1,0:T(8,128)(2,1)S(1)} %collective-permute-done.7.refs_1_.refs_5_), channel_id=1, source_target_pairs={{0,64},{4,12},{1,65},{5,13},{2,66},{6,14},{3,67},{7,15},{32,96},{3... | collective-permute-start | bytes 1572872 | tf_op jit(solution)/shard_map/ppermute | solution.py:40
  38.1 9.2 %collective-permute-start.14 = (bf16[256,1024]{1,0:T(8,128)(2,1)S(1)}, bf16[256,1024]{1,0:T(8,128)(2,1)S(1)}, u32[]{:S(2)}, u32[]{:S(2)}) collective-permute-start(bf16[256,1024]{1,0:T(8,128)(2,1)S(1)} %collective-permute-done.11.refs_6_), channel_id=1, source_target_pairs={{0,4},{4,0},{1,5},{5,1},{2,6},{6,2},{3,7},{7,3},{32,36},{36,32},{3... | collective-permute-start | bytes 1572872 | tf_op jit(solution)/shard_map/ppermute | solution.py:44
  40.7 21.9 %collective-permute-start.21 = (bf16[128,1024]{1,0:T(8,128)(2,1)S(1)}, bf16[128,1024]{1,0:T(8,128)(2,1)S(1)}, u32[]{:S(2)}, u32[]{:S(2)}) collective-permute-start(bf16[128,1024]{1,0:T(8,128)(2,1)S(1)} %shard_map.74.refs_4_), channel_id=1, source_target_pairs={{3,0},{0,1},{1,2},{2,3},{7,4},{4,5},{5,6},{6,7},{11,8},{8,9},{9,10... | collective-permute-start | bytes 786440 | tf_op jit(solution)/shard_map/ppermute | solution.py:244
  40.9 11.4 %collective-permute-start.13 = (bf16[256,1024]{1,0:T(8,128)(2,1)S(1)}, bf16[256,1024]{1,0:T(8,128)(2,1)S(1)}, u32[]{:S(2)}, u32[]{:S(2)}) collective-permute-start(bf16[256,1024]{1,0:T(8,128)(2,1)S(1)} %collective-permute-done.12.refs_8_), channel_id=1, source_target_pairs={{0,4},{4,0},{1,5},{5,1},{2,6},{6,2},{3,7},{7,3},{32,36},{36,32},{3... | collective-permute-start | bytes 1572872 | tf_op jit(solution)/shard_map/ppermute | solution.py:44
  53.6 4.9 %collective-permute-start.17 = (f32[8,128]{1,0:T(8,128)S(1)}, f32[8,128]{1,0:T(8,128)S(1)}, u32[]{:S(2)}, u32[]{:S(2)}) collective-permute-start(f32[8,128]{1,0:T(8,128)S(1)} %get-tuple-element.13.refs_4_), channel_id=1, source_target_pairs={{0,192},{4,28},{1,193},{5,29},{2,194},{6,30},{3,195},{7,31},{32,22... | collective-permute-start | bytes 12296 | tf_op jit(solution)/shard_map/ppermute | solution.py:40
  58.6 3.6 %collective-permute-start.18 = (f32[4,128]{1,0:T(4,128)S(1)}, f32[4,128]{1,0:T(4,128)S(1)}, u32[]{:S(2)}, u32[]{:S(2)}) collective-permute-start(f32[4,128]{1,0:T(4,128)S(1)} %get-tuple-element.15), channel_id=1, source_target_pairs={{0,64},{4,12},{1,65},{5,13},{2,66},{6,14},{3,67},{7,15},{32,96},{3... | collective-permute-start | bytes 6152 | tf_op jit(solution)/shard_map/ppermute | solution.py:40
  62.1 4.8 %collective-permute-start.19 = (f32[2,128]{1,0:T(2,128)S(1)}, f32[2,128]{1,0:T(2,128)S(1)}, u32[]{:S(2)}, u32[]{:S(2)}) collective-permute-start(f32[2,128]{1,0:T(2,128)S(1)} %get-tuple-element.17), channel_id=1, source_target_pairs={{0,24},{4,196},{1,25},{5,197},{2,26},{6,198},{3,27},{7,199},{32,56... | collective-permute-start | bytes 3080 | tf_op jit(solution)/shard_map/ppermute | solution.py:40
  63.5 3.6 %collective-permute-start.22 = (f32[1,128]{1,0:T(1,128)S(1)}, f32[1,128]{1,0:T(1,128)S(1)}, u32[]{:S(2)}, u32[]{:S(2)}) collective-permute-start(f32[1,128]{1,0:T(1,128)S(1)} %get-tuple-element.20), channel_id=1, source_target_pairs={{1,0},{2,1},{3,2},{0,3},{5,4},{6,5},{7,6},{4,7},{9,8},{10,9},{11,1... | collective-permute-start | bytes 1544 | tf_op jit(solution)/shard_map/ppermute | solution.py:244
  66.9 3.5 %collective-permute-start.20 = (f32[1,128]{1,0:T(1,128)S(1)}, f32[1,128]{1,0:T(1,128)S(1)}, u32[]{:S(2)}, u32[]{:S(2)}) collective-permute-start(f32[1,128]{1,0:T(1,128)S(1)} %get-tuple-element.19), channel_id=1, source_target_pairs={{0,8},{4,68},{1,9},{5,69},{2,10},{6,70},{3,11},{7,71},{32,40},{36,... | collective-permute-start | bytes 1544 | tf_op jit(solution)/shard_map/ppermute | solution.py:40
  (4 other events, 27.9 us)
